TPU v7x, 32 devices: a whole 2x2x4 slice. The times are simulated.
32 devices in a mesh: row: 4 (over y, x), col: 8 (over z, core).
Axes of the slice: x: 2, y: 2, z: 4, core: 2. Of those that a mesh axis runs over, the one named last changes fastest.
Arguments:
- chol: bfloat16 [6000, 8192], P('row', 'col'), may hold values from -1.75 to 1.75
- amplitudes: bfloat16 [8192, 4096], P('col', 'row'), may hold values from -0.0625 to 0.0625
- pair_offsets: int32 [4], replicated, may hold values from 0 to 8064
Outputs:
- residual: float32 [512, 4096], P('col', 'row')
All inputs are finite; a program needn't handle non-finite values.
Results may differ from a plain program's by a relative error of at most 0.003.
Values may be sent and summed in bfloat16 or wider, within the bound.
No kernel may reach another device: no remote copies, remote signals or barrier semaphores. Data moves between devices by JAX's collectives and lax.ppermute only.
A program may use at most 64 MiB of HBM per device.

v0:
```python
import functools

import jax
import jax.numpy as jnp
from jax import lax
from jax.experimental import pallas as pl
from jax.experimental.pallas import tpu as pltpu
from jax.sharding import PartitionSpec as P

AB_TILE = 128
SPLIT = (5, 3)
LANES = 128
PAD = 16
AXES = ("row", "col")
VMEM = pltpu.CompilerParams(vmem_limit_bytes=20 * 1024 * 1024)


def pairs(rows, cols, target):
    listed = []
    for row in range(rows):
        for col in range(cols):
            to = target(row, col // 2, col % 2)
            listed.append((row * cols + col, to[0] * cols + to[1] * 2 + to[2]))
    return listed


def entry(offsets, group, span, index):
    low = group * span
    seen = jnp.int32(0)
    block = jnp.int32(0)
    for b in range(offsets.shape[0]):
        start = offsets[b]
        here = ((start < low + span) & (start + (AB_TILE - 1) >= low)).astype(jnp.int32)
        block = jnp.where((here == 1) & (seen == index), b, block)
        seen = seen + here
    return block, seen > index


def most_of(offsets, places, width):
    most = jnp.int32(0)
    for place in range(places):
        low = place * 2 * width
        seen = jnp.int32(0)
        for b in range(offsets.shape[0]):
            here = (offsets[b] < low + 2 * width) & (offsets[b] + (AB_TILE - 1) >= low)
            seen = seen + here.astype(jnp.int32)
        most = jnp.maximum(most, seen)
    return most


def pick_kernel(paired, base, part, share, offsets, chol, keep, give, *refs):
    *most, held, done = refs
    cap, unit, depth = keep.shape
    width = chol.shape[1]
    col = lax.axis_index("col")
    chip, core = lax.div(col, 2), lax.rem(col, 2)
    window = 2 * AB_TILE
    t = lax.broadcasted_iota(jnp.int32, (unit, window), 0)
    lane = lax.broadcasted_iota(jnp.int32, (unit, window), 1)
    place = lax.div(t, part) * share + base + lax.rem(t, part)
    jobs = []
    for slot in range(cap):
        for ref, parity in ((give, 1 - core), (keep, core)):
            if paired:
                index = 2 * lax.rem(chip + slot, 2) + parity
                block, there = entry(offsets, lax.div(chip, 2), 4 * width, index)
            else:
                block, there = entry(offsets, chip, 2 * width, parity)
            start = offsets[block] - col * width
            use = there & (start > -AB_TILE) & (start < width)
            left = jnp.clip(lax.shift_right_arithmetic(start, 7), 0, width // AB_TILE - 2)
            left = pl.multiple_of(left * AB_TILE, AB_TILE)
            at = len(jobs)
            copy = pltpu.make_async_copy(chol.at[:, pl.ds(left, window)], held.at[at], done.at[at])
            pl.when(use)(copy.start)
            jobs.append((use, copy, ref, slot, start - left))
    for at, (use, copy, ref, slot, start) in enumerate(jobs):

        @pl.when(use)
        def _():
            hit = (lane == place + start).astype(jnp.float32).astype(jnp.bfloat16)
            copy.wait()
            ref[slot] = lax.dot_general(
                hit, held[at], (((1,), (1,)), ((), ())), preferred_element_type=jnp.float32
            ).astype(jnp.bfloat16)

        @pl.when(jnp.logical_not(use))
        def _():
            ref[slot] = jnp.zeros((unit, depth), jnp.bfloat16)

    for ref in most:
        ref[0] = most_of(offsets, lax.axis_size("col") // 2, width)


def integrals_kernel(places, paired, offsets, *refs):
    mine, other = refs[:places], refs[places : 2 * places]
    chol, block_out, factors = refs[2 * places :]
    unit, depth = mine[0].shape[1:]
    width = chol.shape[1]
    col = lax.axis_index("col")
    chip, core = lax.div(col, 2), lax.rem(col, 2)
    factors[...] = jnp.zeros_like(factors)
    for j in range(places):
        source = lax.bitwise_xor(chip, j)
        group = lax.div(source, 2) if paired else source
        span = 4 * width if paired else 2 * width
        first = 2 * lax.rem(source, 2) if paired else 0
        for held, parity in ((mine, core), (other, 1 - core)):
            block, there = entry(offsets, group, span, first + parity)

            @pl.when(there)
            def _():
                at = pl.ds(pl.multiple_of(block * unit, unit), unit)
                factors[at, :] += held[j][0]

    height = factors.shape[0]
    value = jnp.dot(factors[...], chol[...], preferred_element_type=jnp.float32)
    top = jnp.max(jnp.max(jnp.abs(value), axis=0, keepdims=True), axis=1, keepdims=True)
    power = jnp.floor(14.0 - jnp.log2(jnp.maximum(top, 1e-30)))
    power = jnp.broadcast_to(jnp.clip(power, -100.0, 100.0), (1, LANES))
    scale = jnp.exp2(power)
    for t in range(width // LANES):
        block_out[t * height : (t + 1) * height, :] = value[:, t * LANES : (t + 1) * LANES] * scale
    block_out[width // LANES * height :, :] = jnp.broadcast_to(power, (PAD, LANES))


def join_kernel(own, came, total):
    end = own.shape[0] - PAD
    first, second = own[end : end + 1, :], came[end : end + 1, :]
    power = jnp.minimum(first, second) - 1.0
    total[:end, :] = own[:end, :] * jnp.exp2(power - first) + came[:end, :] * jnp.exp2(power - second)
    total[end:, :] = jnp.broadcast_to(power, (PAD, LANES))


def residual_kernel(own, came, amplitudes, keep, *refs):
    *gives, block, result = refs
    core = lax.rem(lax.axis_index("col"), 2)
    places, part, _ = keep.shape
    end = own.shape[0] - PAD
    height, width = block.shape
    first, second = jnp.exp2(-own[end : end + 1, :]), jnp.exp2(-came[end : end + 1, :])
    for t in range(width // LANES):
        rows = slice(t * height, (t + 1) * height)
        value = own[rows, :] * first + came[rows, :] * second
        block[:, t * LANES : (t + 1) * LANES] = value.astype(jnp.bfloat16)
    result[...] = jnp.dot(block[...], amplitudes[...], preferred_element_type=jnp.float32)
    for p in range(places):
        keep[p] = result[pl.ds(pl.multiple_of(p * 2 * part + core * part, 8), part), :]
        base = p * 2 * part + (1 - core) * part
        for give in gives:
            give[p] = result[pl.ds(pl.multiple_of(base, 8), give.shape[1]), :]
            base += give.shape[1]


def split_kernel(keep, *refs):
    count = len(refs) - keep.shape[0]
    came, own, gives = refs[:count], refs[count], refs[count + 1 :]
    chip = lax.div(lax.axis_index("col"), 2)
    base = 0
    for piece in came:
        rows = slice(base, base + piece.shape[1])
        own[rows, :] = keep[chip, rows, :] + piece[chip]
        for j, give in enumerate(gives, 1):
            to = lax.bitwise_xor(chip, j)
            give[rows, :] = (keep[to, rows, :] + piece[to]).astype(jnp.bfloat16)
        base += piece.shape[1]


def final_kernel(terms, *refs):
    out = refs[-1]
    base = 0
    for h in range(len(SPLIT)):
        group = refs[h * terms : (h + 1) * terms]
        value = group[0][...]
        for ref in group[1:]:
            value = value + ref[...].astype(jnp.float32)
        out[base : base + value.shape[0], :] = value
        base += value.shape[0]


def call(kernel, outs, smem, *args, scratch=(), flops=0, memory=pltpu.VMEM):
    size = sum(a.size * a.dtype.itemsize for a in args)
    place = lambda o: pl.BlockSpec(memory_space=pltpu.SMEM if o.dtype == jnp.int32 else pltpu.VMEM)
    return pl.pallas_call(
        kernel,
        out_shape=outs,
        out_specs=jax.tree.map(place, outs),
        in_specs=[pl.BlockSpec(memory_space=pltpu.SMEM)] * smem
        + [pl.BlockSpec(memory_space=memory)] * (len(args) - smem),
        scratch_shapes=list(scratch),
        compiler_params=VMEM,
        cost_estimate=pl.CostEstimate(flops=flops, bytes_accessed=size, transcendentals=0),
    )(*args)


def make(rows, cols):
    places = cols // 2
    bits = 2
    swap_core = pairs(rows, cols, lambda r, z, k: (r, z, 1 - k))
    in_plane = [
        pairs(rows, cols, lambda r, z, k, j=j: (r ^ (1 << (j if k == 0 else bits - 1 - j)), z, k))
        for j in range(bits)
    ]
    jumps = [pairs(rows, cols, lambda r, z, k, j=j: (r, z ^ j, k)) for j in range(places)]

    def on_device(chol, amplitudes, pair_offsets):
        depth, width = chol.shape
        columns = amplitudes.shape[1]
        blocks = pair_offsets.shape[0]
        share = blocks * AB_TILE // cols
        parts = [share * eighths // 8 for eighths in SPLIT]

        def picked(h, offsets, paired=False, most=()):
            cap = 2 if paired else 1
            held = jax.ShapeDtypeStruct((cap, AB_TILE // share * parts[h], depth), jnp.bfloat16)
            keep, give, *most = call(
                functools.partial(pick_kernel, paired, sum(parts[:h]), parts[h], share),
                (held, held, *most),
                1,
                offsets,
                chol,
                scratch=[
                    pltpu.VMEM((2 * cap, depth, 2 * AB_TILE), jnp.bfloat16),
                    pltpu.SemaphoreType.DMA((2 * cap,)),
                ],
                memory=pl.ANY,
            )
            return (keep + lax.ppermute(give, AXES, swap_core), *most)

        def gathered(h, offsets):
            (both,) = picked(h, offsets, True)
            return both[:1] + lax.ppermute(both[1:], AXES, jumps[1])

        def rest(paired, own):
            def jump(own, j):
                return lax.ppermute(own, AXES, jumps[j])

            def across(m):
                return lax.ppermute(m, AXES, swap_core)

            def integrals(mine, other):
                height = blocks * mine[0].shape[1]
                return call(
                    functools.partial(integrals_kernel, places, paired),
                    jax.ShapeDtypeStruct((height * width // LANES + PAD, LANES), jnp.float32),
                    1,
                    pair_offsets,
                    *mine,
                    *other,
                    chol,
                    scratch=[pltpu.VMEM((height, depth), jnp.bfloat16)],
                    flops=2 * height * depth * width,
                )

            def swap(block, j):
                came = lax.ppermute(block.astype(jnp.float16), AXES, in_plane[j])
                return came.astype(jnp.float32)

            def join(block, came):
                return call(join_kernel, jax.ShapeDtypeStruct(block.shape, jnp.float32), 0, block, came)

            def residual(block, came, *pieces):
                part = sum(pieces)
                height = places * 2 * part
                keep, *gives = call(
                    residual_kernel,
                    [jax.ShapeDtypeStruct((places, r, columns), jnp.float32) for r in (part, *pieces)],
                    0,
                    block,
                    came,
                    amplitudes,
                    scratch=[
                        pltpu.VMEM((height, width), jnp.bfloat16),
                        pltpu.VMEM((height, columns), jnp.float32),
                    ],
                    flops=2 * height * width * columns,
                )
                return keep, [across(g) for g in gives]

            def split(keep, got):
                part = keep.shape[1]
                return call(
                    split_kernel,
                    (jax.ShapeDtypeStruct((part, columns), jnp.float32),)
                    + (jax.ShapeDtypeStruct((part, columns), jnp.bfloat16),) * (places - 1),
                    0,
                    keep,
                    *got,
                )

            def deliver(gives):
                return [lax.ppermute(g, AXES, jumps[j]) for j, g in enumerate(gives, 1)]

            after = lax.optimization_barrier
            one, two = after((jump(own, 1), jump(own, 2)))
            three = jump(two, 1)
            offsets, _ = after((pair_offsets, (one, two)))
            mine = [own, one, two]
            other = [across(m) for m in mine]
            own = gathered(1, offsets) if paired else picked(1, offsets)[0]
            own, three, *other = after((own, three, *other))
            block = integrals([*mine, three], [*other, across(three)])
            two, one = jump(own, 2), jump(own, 1)
            came = swap(block, 0)
            came, two, one = after((came, two, one))
            block = join(block, came)
            two, _ = after((two, block))
            three = jump(two, 1)
            came = swap(block, 1)
            mine = [own, one, two]
            second = integrals([*mine, three], [across(m) for m in [*mine, three]])
            second, came = after((second, came))
            keep, got = residual(block, came, 16, 16, parts[0] - 32)
            came = swap(second, 0)
            sums, *gives = split(keep, got)
            second = join(second, came)
            second, sums, *gives = after((second, sums, *gives))
            done = [sums] + deliver(gives)
            came, *done = after((swap(second, 1), *done))
            sums, *gives = split(*residual(second, came, parts[1]))
            done += [sums] + deliver(gives)
            return call(
                functools.partial(final_kernel, places),
                jax.ShapeDtypeStruct((share, columns), jnp.float32),
                0,
                *done,
            )

        own, most = picked(0, pair_offsets, False, (jax.ShapeDtypeStruct((1,), jnp.int32),))
        return lax.cond(
            most[0] > 2,
            lambda own: rest(True, gathered(0, pair_offsets)),
            lambda own: rest(False, own),
            own,
        )

    return on_device


def simple(chol, amplitudes, pair_offsets):
    width = chol.shape[1]
    rows = (pair_offsets[:, None] + jnp.arange(AB_TILE, dtype=jnp.int32)[None, :]).reshape(-1)
    local = lax.axis_index("col") * width + jnp.arange(width, dtype=jnp.int32)
    selector = (local[:, None] == rows[None, :]).astype(jnp.bfloat16)
    picked = jnp.dot(chol, selector, preferred_element_type=jnp.float32)
    factors = lax.psum(picked.astype(jnp.bfloat16), "col")
    block = jnp.dot(factors.T, chol, preferred_element_type=jnp.float32)
    block = lax.psum(block, "row").astype(jnp.bfloat16)
    return lax.psum_scatter(
        jnp.dot(block, amplitudes, preferred_element_type=jnp.float32),
        "col",
        scatter_dimension=0,
        tiled=True,
    )


def solution(mesh):
    rows, cols = mesh.shape["row"], mesh.shape["col"]
    body = make(rows, cols) if (rows, cols) == (4, 8) else simple
    return jax.shard_map(
        body,
        mesh=mesh,
        in_specs=(P("row", "col"), P("col", "row"), P()),
        out_specs=P("col", "row"),
        check_vma=False,
    )
```

profile of v0, /device:TPU:0, one launch (start us, length us, event | category | flops | bytes accessed | tf_op | source)
XLA Modules:
  0.0 85.3 jit_solution(12214653473360009029)
XLA Ops:
  0.0 3.0 %shard_map.39 = (bf16[1,80,1500]{2,1,0:T(8,128)(2,1)S(1)}, bf16[1,80,1500]{2,1,0:T(8,128)(2,1)S(1)}, s32[1]{0:T(128)}) custom-call(s32[4]{0:T(128)} %offsets.1, bf16[1500,1024]{1,0:T(8,128)(2,1)} %chol.1), custom_call_target="tpu_custom_call" | custom-call | bytes 3072016 | tf_op jit(solution)/shard_map/pallas_call | solution.py:184
  3.0 0.1 collective-permute-start.61
  3.7 0.8 collective-permute-done.61
  4.6 80.0 %conditional.1 = (f32[64,1024]{1,0:T(8,128)S(1)}) conditional(s32[]{:T(128)} %bitcast, (bf16[1,80,1500]{2,1,0:T(8,128)(2,1)S(1)}, bf16[1,80,1500]{2,1,0:T(8,128)(2,1)S(1)}, s32[4]{0:T(128)S(1)}, bf16[1500,1024]{1,0:T(8,128)(2,1)S(1)}, bf16[1024,1024]{1,0:T(8,128)(2,1)}) %tuple.36, (s32[4]{0:T(128)S(1)}, bf16[1500,1024]{1,0:T(8,128)(2,1)S(1)}, ...), branch_computations={%region_0.0_spmd, %region_1.0_spmd} | conditional | flops 2649295360 | bytes 85637480 | solution.py:330
  4.6 0.1 add.13.refs_0_
  4.7 2.5 %collective-permute-start.1 = (bf16[1,80,1500]{2,1,0:T(8,128)(2,1)S(1)}, bf16[1,80,1500]{2,1,0:T(8,128)(2,1)S(1)}, u32[]{:S(2)}, u32[]{:S(2)}) collective-permute-start(bf16[1,80,1500]{2,1,0:T(8,128)(2,1)S(1)} %add.13.refs_0_), channel_id=1, source_target_pairs={{0,4},{1,5},{2,6},{3,7},{4,0},{5,1},{6,2},{7,3},{8,12},{9,13},{10,... | collective-permute-start | bytes 720008 | tf_op jit(solution)/shard_map/cond/branch_0_fun/ppermute | solution.py:236
  7.2 2.6 %collective-permute-start = (bf16[1,80,1500]{2,1,0:T(8,128)(2,1)S(1)}, bf16[1,80,1500]{2,1,0:T(8,128)(2,1)S(1)}, u32[]{:S(2)}, u32[]{:S(2)}) collective-permute-start(bf16[1,80,1500]{2,1,0:T(8,128)(2,1)S(1)} %add.13.refs_0_), channel_id=1, source_target_pairs={{0,2},{1,3},{2,0},{3,1},{4,6},{5,7},{6,4},{7,5},{8,10},{9,11},{10,... | collective-permute-start | bytes 720008 | tf_op jit(solution)/shard_map/cond/branch_0_fun/ppermute | solution.py:236
  9.8 9.0 %collective-permute-done.1.refs_2_ = bf16[1,80,1500]{2,1,0:T(8,128)(2,1)S(1)} collective-permute-done((bf16[1,80,1500]{2,1,0:T(8,128)(2,1)S(1)}, bf16[1,80,1500]{2,1,0:T(8,128)(2,1)S(1)}, u32[]{:S(2)}, u32[]{:S(2)}) %collective-permute-start.1) | collective-permute-done | bytes 240032 | tf_op jit(solution)/shard_map/cond/branch_0_fun/ppermute | solution.py:236
  18.9 0.5 collective-permute-start.6
  19.4 1.6 %collective-permute-start.3 = (bf16[1,80,1500]{2,1,0:T(8,128)(2,1)S(1)}, bf16[1,80,1500]{2,1,0:T(8,128)(2,1)S(1)}, u32[]{:S(2)}, u32[]{:S(2)}) collective-permute-start(bf16[1,80,1500]{2,1,0:T(8,128)(2,1)S(1)} %collective-permute-done.1.refs_2_), channel_id=1, source_target_pairs={{0,2},{1,3},{2,0},{3,1},{4,6},{5,7},{6,4},{7,5},{8,10},{9,11},{10,... | collective-permute-start | bytes 720008 | tf_op jit(solution)/shard_map/cond/branch_0_fun/ppermute | solution.py:236
  21.0 1.1 %branch_0_fun.10 = (bf16[1,48,1500]{2,1,0:T(8,128)(2,1)S(1)}, bf16[1,48,1500]{2,1,0:T(8,128)(2,1)S(1)}) custom-call(s32[4]{0:T(128)S(1)} %get-tuple-element.30.offsets, bf16[1500,1024]{1,0:T(8,128)(2,1)S(1)} %get-tuple-element.31.chol.refs_8_), custom_call_target="tpu_custom_call" | custom-call | bytes 3072016 | tf_op jit(solution)/shard_map/cond/branch_0_fun/pallas_call | solution.py:184
  22.1 0.1 collective-permute-start.2
  22.2 1.4 %collective-permute-done.2 = bf16[1,48,1500]{2,1,0:T(8,128)(2,1)S(1)} collective-permute-done((bf16[1,48,1500]{2,1,0:T(8,128)(2,1)S(1)}, bf16[1,48,1500]{2,1,0:T(8,128)(2,1)S(1)}, u32[]{:S(2)}, u32[]{:S(2)}) %collective-permute-start.2) | collective-permute-done | bytes 144032 | tf_op jit(solution)/shard_map/cond/branch_0_fun/ppermute | solution.py:228
  23.6 3.6 %collective-permute-done.3.refs_3_ = bf16[1,80,1500]{2,1,0:T(8,128)(2,1)S(1)} collective-permute-done((bf16[1,80,1500]{2,1,0:T(8,128)(2,1)S(1)}, bf16[1,80,1500]{2,1,0:T(8,128)(2,1)S(1)}, u32[]{:S(2)}, u32[]{:S(2)}) %collective-permute-start.3) | collective-permute-done | bytes 240032 | tf_op jit(solution)/shard_map/cond/branch_0_fun/ppermute | solution.py:236
  27.3 1.5 %collective-permute-done.7.refs_7_ = bf16[1,80,1500]{2,1,0:T(8,128)(2,1)S(1)} collective-permute-done((bf16[1,80,1500]{2,1,0:T(8,128)(2,1)S(1)}, bf16[1,80,1500]{2,1,0:T(8,128)(2,1)S(1)}, u32[]{:S(2)}, u32[]{:S(2)}) %collective-permute-start.7) | collective-permute-done | bytes 240032 | tf_op jit(solution)/shard_map/cond/branch_0_fun/ppermute | solution.py:239
  28.8 2.2 %branch_0_fun.11.own = f32[2576,128]{1,0:T(8,128)S(1)} custom-call(s32[4]{0:T(128)S(1)} %get-tuple-element.30.offsets, bf16[1,80,1500]{2,1,0:T(8,128)(2,1)S(1)} %add.13.refs_0_, bf16[1,80,1500]{2,1,0:T(8,128)(2,1)S(1)} %collective-permute-done.refs_1_, bf16[1,80,1500]{2,1,0:T(8,128)(2,1)S(1)} %collective-permute-done.1.refs_2_, ...), custom_call_target="tpu_custom_call" | custom-call | flops 983040000 | bytes 4992016 | tf_op jit(solution)/shard_map/cond/branch_0_fun/pallas_call | solution.py:184
  31.0 0.1 convert_element_type.36
  31.1 3.0 %collective-permute-start.8 = (f16[2576,128]{1,0:T(8,128)(2,1)S(1)}, f16[2576,128]{1,0:T(8,128)(2,1)S(1)}, u32[]{:S(2)}, u32[]{:S(2)}) collective-permute-start(f16[2576,128]{1,0:T(8,128)(2,1)S(1)} %convert_element_type.36), channel_id=1, source_target_pairs={{0,8},{1,17},{2,10},{3,19},{4,12},{5,21},{6,14},{7,23},{8,0},{9,25... | collective-permute-start | bytes 1978376 | tf_op jit(solution)/shard_map/cond/branch_0_fun/ppermute | solution.py:256
  34.1 0.3 collective-permute-start.10
  34.4 3.1 %collective-permute-start.9 = (bf16[1,48,1500]{2,1,0:T(8,128)(2,1)S(1)}, bf16[1,48,1500]{2,1,0:T(8,128)(2,1)S(1)}, u32[]{:S(2)}, u32[]{:S(2)}) collective-permute-start(bf16[1,48,1500]{2,1,0:T(8,128)(2,1)S(1)} %add.14.refs_0_), channel_id=1, source_target_pairs={{0,4},{1,5},{2,6},{3,7},{4,0},{5,1},{6,2},{7,3},{8,12},{9,13},{10,... | collective-permute-start | bytes 432008 | tf_op jit(solution)/shard_map/cond/branch_0_fun/ppermute | solution.py:236
  37.5 5.2 %collective-permute-done.8 = f16[2576,128]{1,0:T(8,128)(2,1)S(1)} collective-permute-done((f16[2576,128]{1,0:T(8,128)(2,1)S(1)}, f16[2576,128]{1,0:T(8,128)(2,1)S(1)}, u32[]{:S(2)}, u32[]{:S(2)}) %collective-permute-start.8) | collective-permute-done | bytes 659488 | tf_op jit(solution)/shard_map/cond/branch_0_fun/ppermute | solution.py:256
  42.7 0.1 convert_element_type.37.came
  42.8 1.5 %collective-permute-done.9.refs_2_ = bf16[1,48,1500]{2,1,0:T(8,128)(2,1)S(1)} collective-permute-done((bf16[1,48,1500]{2,1,0:T(8,128)(2,1)S(1)}, bf16[1,48,1500]{2,1,0:T(8,128)(2,1)S(1)}, u32[]{:S(2)}, u32[]{:S(2)}) %collective-permute-start.9) | collective-permute-done | bytes 144032 | tf_op jit(solution)/shard_map/cond/branch_0_fun/ppermute | solution.py:236
  44.3 0.2 branch_0_fun.12.own
  44.5 0.1 convert_element_type.38
  44.6 0.6 collective-permute-start.16
  45.2 0.3 collective-permute-start.11
  45.5 0.3 collective-permute-start.12
  45.9 0.2 collective-permute-start.14
  46.1 0.3 collective-permute-start.13
  46.4 5.2 %collective-permute-done.11.refs_3_ = bf16[1,48,1500]{2,1,0:T(8,128)(2,1)S(1)} collective-permute-done((bf16[1,48,1500]{2,1,0:T(8,128)(2,1)S(1)}, bf16[1,48,1500]{2,1,0:T(8,128)(2,1)S(1)}, u32[]{:S(2)}, u32[]{:S(2)}) %collective-permute-start.11) | collective-permute-done | bytes 144032 | tf_op jit(solution)/shard_map/cond/branch_0_fun/ppermute | solution.py:236
  51.6 1.3 %collective-permute-done.15.refs_7_ = bf16[1,48,1500]{2,1,0:T(8,128)(2,1)S(1)} collective-permute-done((bf16[1,48,1500]{2,1,0:T(8,128)(2,1)S(1)}, bf16[1,48,1500]{2,1,0:T(8,128)(2,1)S(1)}, u32[]{:S(2)}, u32[]{:S(2)}) %collective-permute-start.15) | collective-permute-done | bytes 144032 | tf_op jit(solution)/shard_map/cond/branch_0_fun/ppermute | solution.py:239
  53.0 1.7 %branch_0_fun.13.own = f32[1552,128]{1,0:T(8,128)S(1)} custom-call(s32[4]{0:T(128)S(1)} %get-tuple-element.30.offsets, bf16[1,48,1500]{2,1,0:T(8,128)(2,1)S(1)} %add.14.refs_0_, bf16[1,48,1500]{2,1,0:T(8,128)(2,1)S(1)} %collective-permute-done.10.refs_1_, bf16[1,48,1500]{2,1,0:T(8,128)(2,1)S(1)} %collective-permute-done.9.refs_2_, ...), custom_call_target="tpu_custom_call" | custom-call | flops 589824000 | bytes 4224016 | tf_op jit(solution)/shard_map/cond/branch_0_fun/pallas_call | solution.py:184
  54.7 0.6 collective-permute-done.16
  55.3 0.1 convert_element_type.39.came
  55.4 0.1 convert_element_type.40
  55.4 1.6 %collective-permute-start.17 = (f16[1552,128]{1,0:T(8,128)(2,1)S(1)}, f16[1552,128]{1,0:T(8,128)(2,1)S(1)}, u32[]{:S(2)}, u32[]{:S(2)}) collective-permute-start(f16[1552,128]{1,0:T(8,128)(2,1)S(1)} %convert_element_type.40), channel_id=1, source_target_pairs={{0,8},{1,17},{2,10},{3,19},{4,12},{5,21},{6,14},{7,23},{8,0},{9,25... | collective-permute-start | bytes 1191944 | tf_op jit(solution)/shard_map/cond/branch_0_fun/ppermute | solution.py:256
  57.0 1.0 %branch_0_fun.15 = (f32[4,40,1024]{2,1,0:T(8,128)S(1)}, f32[4,16,1024]{2,1,0:T(8,128)S(1)}, f32[4,16,1024]{2,1,0:T(8,128)S(1)}, f32[4,8,1024]{2,1,0:T(8,128)S(1)}) custom-call(f32[2576,128]{1,0:T(8,128)S(1)} %branch_0_fun.12.own, f32[2576,128]{1,0:T(8,128)S(1)} %convert_element_type.39.came, bf16[1024,1024]{1,0:T(8,128)(2,1)S(1)} %copy-done.1), custom_call_target="tpu_custom_call" | custom-call | flops 671088640 | bytes 4734976 | tf_op jit(solution)/shard_map/cond/branch_0_fun/pallas_call | solution.py:184
  58.0 0.1 collective-permute-start.18
  58.1 0.5 collective-permute-start.19
  58.6 0.1 collective-permute-start.20
  58.7 1.5 %collective-permute-done.20.refs_2_ = f32[4,8,1024]{2,1,0:T(8,128)S(1)} collective-permute-done((f32[4,8,1024]{2,1,0:T(8,128)S(1)}, f32[4,8,1024]{2,1,0:T(8,128)S(1)}, u32[]{:S(2)}, u32[]{:S(2)}) %collective-permute-start.20) | collective-permute-done | bytes 131104 | tf_op jit(solution)/shard_map/cond/branch_0_fun/ppermute | solution.py:239
  60.2 0.1 branch_0_fun.16
  60.3 3.1 %collective-permute-done.17 = f16[1552,128]{1,0:T(8,128)(2,1)S(1)} collective-permute-done((f16[1552,128]{1,0:T(8,128)(2,1)S(1)}, f16[1552,128]{1,0:T(8,128)(2,1)S(1)}, u32[]{:S(2)}, u32[]{:S(2)}) %collective-permute-start.17) | collective-permute-done | bytes 397344 | tf_op jit(solution)/shard_map/cond/branch_0_fun/ppermute | solution.py:256
  63.4 0.1 branch_0_fun.14.own
  63.5 0.1 convert_element_type.42
  63.6 0.6 collective-permute-start.21
  64.2 0.3 collective-permute-start.22
  64.5 3.1 %collective-permute-start.23 = (bf16[40,1024]{1,0:T(8,128)(2,1)S(1)}, bf16[40,1024]{1,0:T(8,128)(2,1)S(1)}, u32[]{:S(2)}, u32[]{:S(2)}) collective-permute-start(bf16[40,1024]{1,0:T(8,128)(2,1)S(1)} %get-tuple-element.57), channel_id=1, source_target_pairs={{0,4},{1,5},{2,6},{3,7},{4,0},{5,1},{6,2},{7,3},{8,12},{9,13},{10,... | collective-permute-start | bytes 245768 | tf_op jit(solution)/shard_map/cond/branch_0_fun/ppermute | solution.py:292
  67.6 1.0 %collective-permute-start.24 = (bf16[40,1024]{1,0:T(8,128)(2,1)S(1)}, bf16[40,1024]{1,0:T(8,128)(2,1)S(1)}, u32[]{:S(2)}, u32[]{:S(2)}) collective-permute-start(bf16[40,1024]{1,0:T(8,128)(2,1)S(1)} %get-tuple-element.58), channel_id=1, source_target_pairs={{0,6},{1,7},{2,4},{3,5},{4,2},{5,3},{6,0},{7,1},{8,14},{9,15},{10,... | collective-permute-start | bytes 245768 | tf_op jit(solution)/shard_map/cond/branch_0_fun/ppermute | solution.py:292
  68.6 2.9 %collective-permute-done.21 = f16[1552,128]{1,0:T(8,128)(2,1)S(1)} collective-permute-done((f16[1552,128]{1,0:T(8,128)(2,1)S(1)}, f16[1552,128]{1,0:T(8,128)(2,1)S(1)}, u32[]{:S(2)}, u32[]{:S(2)}) %collective-permute-start.21) | collective-permute-done | bytes 397344 | tf_op jit(solution)/shard_map/cond/branch_0_fun/ppermute | solution.py:256
  71.5 0.5 collective-permute-done.23.refs_2_
  72.0 1.8 %collective-permute-done.24.refs_3_ = bf16[40,1024]{1,0:T(8,128)(2,1)S(1)} collective-permute-done((bf16[40,1024]{1,0:T(8,128)(2,1)S(1)}, bf16[40,1024]{1,0:T(8,128)(2,1)S(1)}, u32[]{:S(2)}, u32[]{:S(2)}) %collective-permute-start.24) | collective-permute-done | bytes 81952 | tf_op jit(solution)/shard_map/cond/branch_0_fun/ppermute | solution.py:292
  73.8 0.7 branch_0_fun.17
  74.5 0.1 collective-permute-start.25
  74.6 1.7 %collective-permute-done.25.refs_0_ = f32[4,24,1024]{2,1,0:T(8,128)S(1)} collective-permute-done((f32[4,24,1024]{2,1,0:T(8,128)S(1)}, f32[4,24,1024]{2,1,0:T(8,128)S(1)}, u32[]{:S(2)}, u32[]{:S(2)}) %collective-permute-start.25) | collective-permute-done | bytes 393248 | tf_op jit(solution)/shard_map/cond/branch_0_fun/ppermute | solution.py:239
  76.4 0.1 collective-permute-start.26
  76.4 1.9 %collective-permute-start.27 = (bf16[24,1024]{1,0:T(8,128)(2,1)S(1)}, bf16[24,1024]{1,0:T(8,128)(2,1)S(1)}, u32[]{:S(2)}, u32[]{:S(2)}) collective-permute-start(bf16[24,1024]{1,0:T(8,128)(2,1)S(1)} %get-tuple-element.68), channel_id=1, source_target_pairs={{0,4},{1,5},{2,6},{3,7},{4,0},{5,1},{6,2},{7,3},{8,12},{9,13},{10,... | collective-permute-start | bytes 147464 | tf_op jit(solution)/shard_map/cond/branch_0_fun/ppermute | solution.py:292
  78.3 2.5 %collective-permute-start.28 = (bf16[24,1024]{1,0:T(8,128)(2,1)S(1)}, bf16[24,1024]{1,0:T(8,128)(2,1)S(1)}, u32[]{:S(2)}, u32[]{:S(2)}) collective-permute-start(bf16[24,1024]{1,0:T(8,128)(2,1)S(1)} %get-tuple-element.69), channel_id=1, source_target_pairs={{0,6},{1,7},{2,4},{3,5},{4,2},{5,3},{6,0},{7,1},{8,14},{9,15},{10,... | collective-permute-start | bytes 147464 | tf_op jit(solution)/shard_map/cond/branch_0_fun/ppermute | solution.py:292
  80.8 0.6 collective-permute-done.26.refs_5_
  81.4 0.8 collective-permute-done.27.refs_6_
  82.3 2.0 %collective-permute-done.28.refs_7_ = bf16[24,1024]{1,0:T(8,128)(2,1)S(1)} collective-permute-done((bf16[24,1024]{1,0:T(8,128)(2,1)S(1)}, bf16[24,1024]{1,0:T(8,128)(2,1)S(1)}, u32[]{:S(2)}, u32[]{:S(2)}) %collective-permute-start.28) | collective-permute-done | bytes 49184 | tf_op jit(solution)/shard_map/cond/branch_0_fun/ppermute | solution.py:292
  84.3 0.1 branch_0_fun.19
  84.6 0.7 copy-done.3
  (26 shorter events, 0.2 us)
Async XLA Ops:
  0.0 4.6 %copy-start.4 = (s32[4]{0:T(128)S(1)}, s32[4]{0:T(128)}, u32[]{:S(2)}) copy-start(s32[4]{0:T(128)} %offsets.1) | copy-start | bytes 52
  0.0 4.6 %copy-start = (bf16[1500,1024]{1,0:T(8,128)(2,1)S(1)}, bf16[1500,1024]{1,0:T(8,128)(2,1)}, u32[]{:S(2)}) copy-start(bf16[1500,1024]{1,0:T(8,128)(2,1)} %chol.1) | copy-start | bytes 9216004
  3.0 1.6 %collective-permute-start.61 = (bf16[1,80,1500]{2,1,0:T(8,128)(2,1)S(1)}, bf16[1,80,1500]{2,1,0:T(8,128)(2,1)S(1)}, u32[]{:S(2)}, u32[]{:S(2)}) collective-permute-start(bf16[1,80,1500]{2,1,0:T(8,128)(2,1)S(1)} %get-tuple-element.120), channel_id=1, source_target_pairs={{0,1},{1,0},{2,3},{3,2},{4,5},{5,4},{6,7},{7,6},{8,9},{9,8},{10,11... | collective-permute-start | bytes 720008 | tf_op jit(solution)/shard_map/ppermute | solution.py:228
  4.7 14.2 %collective-permute-start.1 = (bf16[1,80,1500]{2,1,0:T(8,128)(2,1)S(1)}, bf16[1,80,1500]{2,1,0:T(8,128)(2,1)S(1)}, u32[]{:S(2)}, u32[]{:S(2)}) collective-permute-start(bf16[1,80,1500]{2,1,0:T(8,128)(2,1)S(1)} %add.13.refs_0_), channel_id=1, source_target_pairs={{0,4},{1,5},{2,6},{3,7},{4,0},{5,1},{6,2},{7,3},{8,12},{9,13},{10,... | collective-permute-start | bytes 720008 | tf_op jit(solution)/shard_map/cond/branch_0_fun/ppermute | solution.py:236
  7.2 11.7 %collective-permute-start = (bf16[1,80,1500]{2,1,0:T(8,128)(2,1)S(1)}, bf16[1,80,1500]{2,1,0:T(8,128)(2,1)S(1)}, u32[]{:S(2)}, u32[]{:S(2)}) collective-permute-start(bf16[1,80,1500]{2,1,0:T(8,128)(2,1)S(1)} %add.13.refs_0_), channel_id=1, source_target_pairs={{0,2},{1,3},{2,0},{3,1},{4,6},{5,7},{6,4},{7,5},{8,10},{9,11},{10,... | collective-permute-start | bytes 720008 | tf_op jit(solution)/shard_map/cond/branch_0_fun/ppermute | solution.py:236
  9.8 13.8 %collective-permute-start.4 = (bf16[1,80,1500]{2,1,0:T(8,128)(2,1)S(1)}, bf16[1,80,1500]{2,1,0:T(8,128)(2,1)S(1)}, u32[]{:S(2)}, u32[]{:S(2)}) collective-permute-start(bf16[1,80,1500]{2,1,0:T(8,128)(2,1)S(1)} %add.13.refs_0_), channel_id=1, source_target_pairs={{0,1},{1,0},{2,3},{3,2},{4,5},{5,4},{6,7},{7,6},{8,9},{9,8},{10,11... | collective-permute-start | bytes 720008 | tf_op jit(solution)/shard_map/cond/branch_0_fun/ppermute | solution.py:239
  18.9 4.7 %collective-permute-start.5 = (bf16[1,80,1500]{2,1,0:T(8,128)(2,1)S(1)}, bf16[1,80,1500]{2,1,0:T(8,128)(2,1)S(1)}, u32[]{:S(2)}, u32[]{:S(2)}) collective-permute-start(bf16[1,80,1500]{2,1,0:T(8,128)(2,1)S(1)} %collective-permute-done.refs_1_), channel_id=1, source_target_pairs={{0,1},{1,0},{2,3},{3,2},{4,5},{5,4},{6,7},{7,6},{8,9},{9,8},{10,11... | collective-permute-start | bytes 720008 | tf_op jit(solution)/shard_map/cond/branch_0_fun/ppermute | solution.py:239
  18.9 4.7 %collective-permute-start.6 = (bf16[1,80,1500]{2,1,0:T(8,128)(2,1)S(1)}, bf16[1,80,1500]{2,1,0:T(8,128)(2,1)S(1)}, u32[]{:S(2)}, u32[]{:S(2)}) collective-permute-start(bf16[1,80,1500]{2,1,0:T(8,128)(2,1)S(1)} %collective-permute-done.1.refs_2_), channel_id=1, source_target_pairs={{0,1},{1,0},{2,3},{3,2},{4,5},{5,4},{6,7},{7,6},{8,9},{9,8},{10,11... | collective-permute-start | bytes 720008 | tf_op jit(solution)/shard_map/cond/branch_0_fun/ppermute | solution.py:239
  19.4 7.9 %collective-permute-start.3 = (bf16[1,80,1500]{2,1,0:T(8,128)(2,1)S(1)}, bf16[1,80,1500]{2,1,0:T(8,128)(2,1)S(1)}, u32[]{:S(2)}, u32[]{:S(2)}) collective-permute-start(bf16[1,80,1500]{2,1,0:T(8,128)(2,1)S(1)} %collective-permute-done.1.refs_2_), channel_id=1, source_target_pairs={{0,2},{1,3},{2,0},{3,1},{4,6},{5,7},{6,4},{7,5},{8,10},{9,11},{10,... | collective-permute-start | bytes 720008 | tf_op jit(solution)/shard_map/cond/branch_0_fun/ppermute | solution.py:236
  22.1 1.4 %collective-permute-start.2 = (bf16[1,48,1500]{2,1,0:T(8,128)(2,1)S(1)}, bf16[1,48,1500]{2,1,0:T(8,128)(2,1)S(1)}, u32[]{:S(2)}, u32[]{:S(2)}) collective-permute-start(bf16[1,48,1500]{2,1,0:T(8,128)(2,1)S(1)} %get-tuple-element.33), channel_id=1, source_target_pairs={{0,1},{1,0},{2,3},{3,2},{4,5},{5,4},{6,7},{7,6},{8,9},{9,8},{10,11... | collective-permute-start | bytes 432008 | tf_op jit(solution)/shard_map/cond/branch_0_fun/ppermute | solution.py:228
  27.3 1.5 %collective-permute-start.7 = (bf16[1,80,1500]{2,1,0:T(8,128)(2,1)S(1)}, bf16[1,80,1500]{2,1,0:T(8,128)(2,1)S(1)}, u32[]{:S(2)}, u32[]{:S(2)}) collective-permute-start(bf16[1,80,1500]{2,1,0:T(8,128)(2,1)S(1)} %collective-permute-done.3.refs_3_), channel_id=1, source_target_pairs={{0,1},{1,0},{2,3},{3,2},{4,5},{5,4},{6,7},{7,6},{8,9},{9,8},{10,11... | collective-permute-start | bytes 720008 | tf_op jit(solution)/shard_map/cond/branch_0_fun/ppermute | solution.py:239
  31.1 11.6 %collective-permute-start.8 = (f16[2576,128]{1,0:T(8,128)(2,1)S(1)}, f16[2576,128]{1,0:T(8,128)(2,1)S(1)}, u32[]{:S(2)}, u32[]{:S(2)}) collective-permute-start(f16[2576,128]{1,0:T(8,128)(2,1)S(1)} %convert_element_type.36), channel_id=1, source_target_pairs={{0,8},{1,17},{2,10},{3,19},{4,12},{5,21},{6,14},{7,23},{8,0},{9,25... | collective-permute-start | bytes 1978376 | tf_op jit(solution)/shard_map/cond/branch_0_fun/ppermute | solution.py:256
  34.1 8.7 %collective-permute-start.10 = (bf16[1,48,1500]{2,1,0:T(8,128)(2,1)S(1)}, bf16[1,48,1500]{2,1,0:T(8,128)(2,1)S(1)}, u32[]{:S(2)}, u32[]{:S(2)}) collective-permute-start(bf16[1,48,1500]{2,1,0:T(8,128)(2,1)S(1)} %add.14.refs_0_), channel_id=1, source_target_pairs={{0,2},{1,3},{2,0},{3,1},{4,6},{5,7},{6,4},{7,5},{8,10},{9,11},{10,... | collective-permute-start | bytes 432008 | tf_op jit(solution)/shard_map/cond/branch_0_fun/ppermute | solution.py:236
  34.4 9.9 %collective-permute-start.9 = (bf16[1,48,1500]{2,1,0:T(8,128)(2,1)S(1)}, bf16[1,48,1500]{2,1,0:T(8,128)(2,1)S(1)}, u32[]{:S(2)}, u32[]{:S(2)}) collective-permute-start(bf16[1,48,1500]{2,1,0:T(8,128)(2,1)S(1)} %add.14.refs_0_), channel_id=1, source_target_pairs={{0,4},{1,5},{2,6},{3,7},{4,0},{5,1},{6,2},{7,3},{8,12},{9,13},{10,... | collective-permute-start | bytes 432008 | tf_op jit(solution)/shard_map/cond/branch_0_fun/ppermute | solution.py:236
  44.6 10.7 %collective-permute-start.16 = (f16[2576,128]{1,0:T(8,128)(2,1)S(1)}, f16[2576,128]{1,0:T(8,128)(2,1)S(1)}, u32[]{:S(2)}, u32[]{:S(2)}) collective-permute-start(f16[2576,128]{1,0:T(8,128)(2,1)S(1)} %convert_element_type.38), channel_id=1, source_target_pairs={{0,16},{1,9},{2,18},{3,11},{4,20},{5,13},{6,22},{7,15},{8,24},{9,1... | collective-permute-start | bytes 1978376 | tf_op jit(solution)/shard_map/cond/branch_0_fun/ppermute | solution.py:256
  45.2 6.4 %collective-permute-start.11 = (bf16[1,48,1500]{2,1,0:T(8,128)(2,1)S(1)}, bf16[1,48,1500]{2,1,0:T(8,128)(2,1)S(1)}, u32[]{:S(2)}, u32[]{:S(2)}) collective-permute-start(bf16[1,48,1500]{2,1,0:T(8,128)(2,1)S(1)} %collective-permute-done.9.refs_2_), channel_id=1, source_target_pairs={{0,2},{1,3},{2,0},{3,1},{4,6},{5,7},{6,4},{7,5},{8,10},{9,11},{10,... | collective-permute-start | bytes 432008 | tf_op jit(solution)/shard_map/cond/branch_0_fun/ppermute | solution.py:236
  45.5 6.1 %collective-permute-start.12 = (bf16[1,48,1500]{2,1,0:T(8,128)(2,1)S(1)}, bf16[1,48,1500]{2,1,0:T(8,128)(2,1)S(1)}, u32[]{:S(2)}, u32[]{:S(2)}) collective-permute-start(bf16[1,48,1500]{2,1,0:T(8,128)(2,1)S(1)} %add.14.refs_0_), channel_id=1, source_target_pairs={{0,1},{1,0},{2,3},{3,2},{4,5},{5,4},{6,7},{7,6},{8,9},{9,8},{10,11... | collective-permute-start | bytes 432008 | tf_op jit(solution)/shard_map/cond/branch_0_fun/ppermute | solution.py:239
  45.9 5.7 %collective-permute-start.14 = (bf16[1,48,1500]{2,1,0:T(8,128)(2,1)S(1)}, bf16[1,48,1500]{2,1,0:T(8,128)(2,1)S(1)}, u32[]{:S(2)}, u32[]{:S(2)}) collective-permute-start(bf16[1,48,1500]{2,1,0:T(8,128)(2,1)S(1)} %collective-permute-done.9.refs_2_), channel_id=1, source_target_pairs={{0,1},{1,0},{2,3},{3,2},{4,5},{5,4},{6,7},{7,6},{8,9},{9,8},{10,11... | collective-permute-start | bytes 432008 | tf_op jit(solution)/shard_map/cond/branch_0_fun/ppermute | solution.py:239
  46.1 5.6 %collective-permute-start.13 = (bf16[1,48,1500]{2,1,0:T(8,128)(2,1)S(1)}, bf16[1,48,1500]{2,1,0:T(8,128)(2,1)S(1)}, u32[]{:S(2)}, u32[]{:S(2)}) collective-permute-start(bf16[1,48,1500]{2,1,0:T(8,128)(2,1)S(1)} %collective-permute-done.10.refs_1_), channel_id=1, source_target_pairs={{0,1},{1,0},{2,3},{3,2},{4,5},{5,4},{6,7},{7,6},{8,9},{9,8},{10,11... | collective-permute-start | bytes 432008 | tf_op jit(solution)/shard_map/cond/branch_0_fun/ppermute | solution.py:239
  51.6 1.4 %collective-permute-start.15 = (bf16[1,48,1500]{2,1,0:T(8,128)(2,1)S(1)}, bf16[1,48,1500]{2,1,0:T(8,128)(2,1)S(1)}, u32[]{:S(2)}, u32[]{:S(2)}) collective-permute-start(bf16[1,48,1500]{2,1,0:T(8,128)(2,1)S(1)} %collective-permute-done.11.refs_3_), channel_id=1, source_target_pairs={{0,1},{1,0},{2,3},{3,2},{4,5},{5,4},{6,7},{7,6},{8,9},{9,8},{10,11... | collective-permute-start | bytes 432008 | tf_op jit(solution)/shard_map/cond/branch_0_fun/ppermute | solution.py:239
  54.7 2.3 %copy-start.1 = (bf16[1024,1024]{1,0:T(8,128)(2,1)S(1)}, bf16[1024,1024]{1,0:T(8,128)(2,1)}, u32[]{:S(2)}) copy-start(bf16[1024,1024]{1,0:T(8,128)(2,1)} %get-tuple-element.45.amplitudes) | copy-start | bytes 6291460 | tf_op jit(solution)/shard_map/cond
  55.4 7.9 %collective-permute-start.17 = (f16[1552,128]{1,0:T(8,128)(2,1)S(1)}, f16[1552,128]{1,0:T(8,128)(2,1)S(1)}, u32[]{:S(2)}, u32[]{:S(2)}) collective-permute-start(f16[1552,128]{1,0:T(8,128)(2,1)S(1)} %convert_element_type.40), channel_id=1, source_target_pairs={{0,8},{1,17},{2,10},{3,19},{4,12},{5,21},{6,14},{7,23},{8,0},{9,25... | collective-permute-start | bytes 1191944 | tf_op jit(solution)/shard_map/cond/branch_0_fun/ppermute | solution.py:256
  58.0 2.2 %collective-permute-start.18 = (f32[4,16,1024]{2,1,0:T(8,128)S(1)}, f32[4,16,1024]{2,1,0:T(8,128)S(1)}, u32[]{:S(2)}, u32[]{:S(2)}) collective-permute-start(f32[4,16,1024]{2,1,0:T(8,128)S(1)} %get-tuple-element.47), channel_id=1, source_target_pairs={{0,1},{1,0},{2,3},{3,2},{4,5},{5,4},{6,7},{7,6},{8,9},{9,8},{10,11... | collective-permute-start | bytes 786440 | tf_op jit(solution)/shard_map/cond/branch_0_fun/ppermute | solution.py:239
  58.1 2.1 %collective-permute-start.19 = (f32[4,16,1024]{2,1,0:T(8,128)S(1)}, f32[4,16,1024]{2,1,0:T(8,128)S(1)}, u32[]{:S(2)}, u32[]{:S(2)}) collective-permute-start(f32[4,16,1024]{2,1,0:T(8,128)S(1)} %get-tuple-element.48), channel_id=1, source_target_pairs={{0,1},{1,0},{2,3},{3,2},{4,5},{5,4},{6,7},{7,6},{8,9},{9,8},{10,11... | collective-permute-start | bytes 786440 | tf_op jit(solution)/shard_map/cond/branch_0_fun/ppermute | solution.py:239
  58.6 1.6 %collective-permute-start.20 = (f32[4,8,1024]{2,1,0:T(8,128)S(1)}, f32[4,8,1024]{2,1,0:T(8,128)S(1)}, u32[]{:S(2)}, u32[]{:S(2)}) collective-permute-start(f32[4,8,1024]{2,1,0:T(8,128)S(1)} %get-tuple-element.49), channel_id=1, source_target_pairs={{0,1},{1,0},{2,3},{3,2},{4,5},{5,4},{6,7},{7,6},{8,9},{9,8},{10,11... | collective-permute-start | bytes 393224 | tf_op jit(solution)/shard_map/cond/branch_0_fun/ppermute | solution.py:239
  63.6 7.9 %collective-permute-start.21 = (f16[1552,128]{1,0:T(8,128)(2,1)S(1)}, f16[1552,128]{1,0:T(8,128)(2,1)S(1)}, u32[]{:S(2)}, u32[]{:S(2)}) collective-permute-start(f16[1552,128]{1,0:T(8,128)(2,1)S(1)} %convert_element_type.42), channel_id=1, source_target_pairs={{0,16},{1,9},{2,18},{3,11},{4,20},{5,13},{6,22},{7,15},{8,24},{9,1... | collective-permute-start | bytes 1191944 | tf_op jit(solution)/shard_map/cond/branch_0_fun/ppermute | solution.py:256
  64.2 7.3 %collective-permute-start.22 = (bf16[40,1024]{1,0:T(8,128)(2,1)S(1)}, bf16[40,1024]{1,0:T(8,128)(2,1)S(1)}, u32[]{:S(2)}, u32[]{:S(2)}) collective-permute-start(bf16[40,1024]{1,0:T(8,128)(2,1)S(1)} %get-tuple-element.56), channel_id=1, source_target_pairs={{0,2},{1,3},{2,0},{3,1},{4,6},{5,7},{6,4},{7,5},{8,10},{9,11},{10,... | collective-permute-start | bytes 245768 | tf_op jit(solution)/shard_map/cond/branch_0_fun/ppermute | solution.py:292
  64.5 7.5 %collective-permute-start.23 = (bf16[40,1024]{1,0:T(8,128)(2,1)S(1)}, bf16[40,1024]{1,0:T(8,128)(2,1)S(1)}, u32[]{:S(2)}, u32[]{:S(2)}) collective-permute-start(bf16[40,1024]{1,0:T(8,128)(2,1)S(1)} %get-tuple-element.57), channel_id=1, source_target_pairs={{0,4},{1,5},{2,6},{3,7},{4,0},{5,1},{6,2},{7,3},{8,12},{9,13},{10,... | collective-permute-start | bytes 245768 | tf_op jit(solution)/shard_map/cond/branch_0_fun/ppermute | solution.py:292
  67.6 6.2 %collective-permute-start.24 = (bf16[40,1024]{1,0:T(8,128)(2,1)S(1)}, bf16[40,1024]{1,0:T(8,128)(2,1)S(1)}, u32[]{:S(2)}, u32[]{:S(2)}) collective-permute-start(bf16[40,1024]{1,0:T(8,128)(2,1)S(1)} %get-tuple-element.58), channel_id=1, source_target_pairs={{0,6},{1,7},{2,4},{3,5},{4,2},{5,3},{6,0},{7,1},{8,14},{9,15},{10,... | collective-permute-start | bytes 245768 | tf_op jit(solution)/shard_map/cond/branch_0_fun/ppermute | solution.py:292
  74.5 1.8 %collective-permute-start.25 = (f32[4,24,1024]{2,1,0:T(8,128)S(1)}, f32[4,24,1024]{2,1,0:T(8,128)S(1)}, u32[]{:S(2)}, u32[]{:S(2)}) collective-permute-start(f32[4,24,1024]{2,1,0:T(8,128)S(1)} %get-tuple-element.65), channel_id=1, source_target_pairs={{0,1},{1,0},{2,3},{3,2},{4,5},{5,4},{6,7},{7,6},{8,9},{9,8},{10,11... | collective-permute-start | bytes 1179656 | tf_op jit(solution)/shard_map/cond/branch_0_fun/ppermute | solution.py:239
  76.4 5.1 %collective-permute-start.26 = (bf16[24,1024]{1,0:T(8,128)(2,1)S(1)}, bf16[24,1024]{1,0:T(8,128)(2,1)S(1)}, u32[]{:S(2)}, u32[]{:S(2)}) collective-permute-start(bf16[24,1024]{1,0:T(8,128)(2,1)S(1)} %get-tuple-element.67), channel_id=1, source_target_pairs={{0,2},{1,3},{2,0},{3,1},{4,6},{5,7},{6,4},{7,5},{8,10},{9,11},{10,... | collective-permute-start | bytes 147464 | tf_op jit(solution)/shard_map/cond/branch_0_fun/ppermute | solution.py:292
  76.4 5.8 %collective-permute-start.27 = (bf16[24,1024]{1,0:T(8,128)(2,1)S(1)}, bf16[24,1024]{1,0:T(8,128)(2,1)S(1)}, u32[]{:S(2)}, u32[]{:S(2)}) collective-permute-start(bf16[24,1024]{1,0:T(8,128)(2,1)S(1)} %get-tuple-element.68), channel_id=1, source_target_pairs={{0,4},{1,5},{2,6},{3,7},{4,0},{5,1},{6,2},{7,3},{8,12},{9,13},{10,... | collective-permute-start | bytes 147464 | tf_op jit(solution)/shard_map/cond/branch_0_fun/ppermute | solution.py:292
  78.3 5.9 %collective-permute-start.28 = (bf16[24,1024]{1,0:T(8,128)(2,1)S(1)}, bf16[24,1024]{1,0:T(8,128)(2,1)S(1)}, u32[]{:S(2)}, u32[]{:S(2)}) collective-permute-start(bf16[24,1024]{1,0:T(8,128)(2,1)S(1)} %get-tuple-element.69), channel_id=1, source_target_pairs={{0,6},{1,7},{2,4},{3,5},{4,2},{5,3},{6,0},{7,1},{8,14},{9,15},{10,... | collective-permute-start | bytes 147464 | tf_op jit(solution)/shard_map/cond/branch_0_fun/ppermute | solution.py:292
  84.6 0.7 copy-start.3
where the time goes:
time: 85.8 us; the launch traced here: 85.3 us
  waiting for transfers between devices  45.2 us (53%)
  starting transfers between devices  27.4 us (32%)
  Pallas kernels  10.2 us (12%)
    ppermute x6, waiting for transfers between devices, jump(): return lax.ppermute(own, AXES, jumps[j])  19.4 us
    ppermute x4, waiting for transfers between devices, swap(): came = lax.ppermute(block.astype(jnp.float16), AXES, in_plane[j])  11.7 us
    ppermute x6, starting transfers between devices, jump(): return lax.ppermute(own, AXES, jumps[j])  10.5 us
    pallas_call x11, Pallas kernels, call(): pl.pallas_call(kernel, out_shape=outs, out_specs=jax.tree.map(place, outs...  10.2 us
    ppermute x6, starting transfers between devices, deliver(): return [lax.ppermute(g, AXES, jumps[j]) for j, g in enumerate(gives, 1)]  8.83 us
    ppermute x12, waiting for transfers between devices, across(): return lax.ppermute(m, AXES, swap_core)  6.1 us
    ppermute x4, starting transfers between devices, swap(): came = lax.ppermute(block.astype(jnp.float16), AXES, in_plane[j])  5.8 us
    ppermute x6, waiting for transfers between devices, deliver(): return [lax.ppermute(g, AXES, jumps[j]) for j, g in enumerate(gives, 1)]  5.75 us
  transfers between devices with their start and end apart: 30, of which 19 were waited for; matrix products, arithmetic and copies ran while one was open for 0% of the time, Pallas kernels for 5%

commit v1 on v0

--- a/solution.py
+++ b/solution.py
@@ -289,7 +289,7 @@
                 )
 
             def deliver(gives):
-                return [lax.ppermute(g, AXES, jumps[j]) for j, g in enumerate(gives, 1)]
+                return [lax.ppermute(g, AXES, jumps[j]) for j, g in reversed(list(enumerate(gives, 1)))]
 
             after = lax.optimization_barrier
             one, two = after((jump(own, 1), jump(own, 2)))
@@ -300,7 +300,7 @@
             own = gathered(1, offsets) if paired else picked(1, offsets)[0]
             own, three, *other = after((own, three, *other))
             block = integrals([*mine, three], [*other, across(three)])
-            two, one = jump(own, 2), jump(own, 1)
+            one, two = jump(own, 1), jump(own, 2)
             came = swap(block, 0)
             came, two, one = after((came, two, one))
             block = join(block, came)
@@ -328,9 +328,9 @@
 
         own, most = picked(0, pair_offsets, False, (jax.ShapeDtypeStruct((1,), jnp.int32),))
         return lax.cond(
-            most[0] > 2,
+            most[0] <= 2,
+            lambda own: rest(False, own),
             lambda own: rest(True, gathered(0, pair_offsets)),
-            lambda own: rest(False, own),
             own,
         )
 

time: 85.8 us -> 85.5 us (level)
  waiting for transfers between devices: 45.2 us -> 47.8 us
  starting transfers between devices: 27.4 us -> 25.2 us
    ppermute x6, waiting for transfers between devices: 19.4 us -> 21.5 us  [jump(): return lax.ppermute(own, AXES, jumps[j])]
    ppermute x4, starting transfers between devices: 5.8 us -> 4.16 us  [swap(): came = lax.ppermute(block.astype(jnp.float16), AXES, in_plane[j])]
    ppermute x4, waiting for transfers between devices: 11.7 us -> 12.8 us  [swap(): came = lax.ppermute(block.astype(jnp.float16), AXES, in_plane[j])]
  transfers between devices with their start and end apart: 30 -> 30, of which waited for: 19 -> 18; matrix products, arithmetic and copies ran while one was open for 0% -> 0% of each run, Pallas kernels for 5% -> 5%
where the time goes in v1:
time: 85.5 us; the launch traced here: 85.8 us
  waiting for transfers between devices  47.8 us (56%)
  starting transfers between devices  25.2 us (29%)
  Pallas kernels  10.3 us (12%)
    ppermute x6, waiting for transfers between devices, jump(): return lax.ppermute(own, AXES, jumps[j])  21.5 us
    ppermute x4, waiting for transfers between devices, swap(): came = lax.ppermute(block.astype(jnp.float16), AXES, in_plane[j])  12.8 us
    pallas_call x11, Pallas kernels, call(): pl.pallas_call(kernel, out_shape=outs, out_specs=jax.tree.map(place, outs...  10.3 us
    ppermute x6, starting transfers between devices, jump(): return lax.ppermute(own, AXES, jumps[j])  10.3 us
    ppermute x6, starting transfers between devices, deliver(): lax.ppermute(g, AXES, jumps[j])  8.84 us
    ppermute x12, waiting for transfers between devices, across(): return lax.ppermute(m, AXES, swap_core)  6.1 us
    ppermute x6, waiting for transfers between devices, deliver(): lax.ppermute(g, AXES, jumps[j])  5.25 us
    ppermute x4, starting transfers between devices, swap(): came = lax.ppermute(block.astype(jnp.float16), AXES, in_plane[j])  4.16 us
  transfers between devices with their start and end apart: 30, of which 18 were waited for; matrix products, arithmetic and copies ran while one was open for 0% of the time, Pallas kernels for 5%

profile of v1, /device:TPU:0, one launch (start us, length us, event | category | flops | bytes accessed | tf_op | source)
XLA Modules:
  0.0 85.8 jit_solution(16035019153277276809)
XLA Ops:
  0.0 3.0 %shard_map.39 = (bf16[1,80,1500]{2,1,0:T(8,128)(2,1)S(1)}, bf16[1,80,1500]{2,1,0:T(8,128)(2,1)S(1)}, s32[1]{0:T(128)}) custom-call(s32[4]{0:T(128)} %offsets.1, bf16[1500,1024]{1,0:T(8,128)(2,1)} %chol.1), custom_call_target="tpu_custom_call" | custom-call | bytes 3072016 | tf_op jit(solution)/shard_map/pallas_call | solution.py:184
  3.0 0.1 collective-permute-start.61
  3.7 0.8 collective-permute-done.61
  4.6 80.5 %conditional.1 = (f32[64,1024]{1,0:T(8,128)S(1)}) conditional(s32[]{:T(128)} %bitcast, (s32[4]{0:T(128)S(1)}, bf16[1500,1024]{1,0:T(8,128)(2,1)S(1)}, bf16[1024,1024]{1,0:T(8,128)(2,1)}) %tuple.36, (bf16[1,80,1500]{2,1,0:T(8,128)(2,1)S(1)}, bf16[1,80,1500]{2,1,0:T(8,128)(2,1)S(1)}, s32[4]{0:T(128)S(1)}, bf16[1500,1024]{1,0:T(8,128)(2,1)S(1)}, ...), branch_computations={%region_0.0_spmd, %region_1.0_spmd} | conditional | flops 2649295360 | bytes 85637480 | solution.py:330
  4.6 0.1 add.17.refs_0_
  4.7 4.0 %collective-permute-start.1 = (bf16[1,80,1500]{2,1,0:T(8,128)(2,1)S(1)}, bf16[1,80,1500]{2,1,0:T(8,128)(2,1)S(1)}, u32[]{:S(2)}, u32[]{:S(2)}) collective-permute-start(bf16[1,80,1500]{2,1,0:T(8,128)(2,1)S(1)} %add.17.refs_0_), channel_id=1, source_target_pairs={{0,4},{1,5},{2,6},{3,7},{4,0},{5,1},{6,2},{7,3},{8,12},{9,13},{10,... | collective-permute-start | bytes 720008 | tf_op jit(solution)/shard_map/cond/branch_1_fun/ppermute | solution.py:236
  8.6 1.2 %collective-permute-start = (bf16[1,80,1500]{2,1,0:T(8,128)(2,1)S(1)}, bf16[1,80,1500]{2,1,0:T(8,128)(2,1)S(1)}, u32[]{:S(2)}, u32[]{:S(2)}) collective-permute-start(bf16[1,80,1500]{2,1,0:T(8,128)(2,1)S(1)} %add.17.refs_0_), channel_id=1, source_target_pairs={{0,2},{1,3},{2,0},{3,1},{4,6},{5,7},{6,4},{7,5},{8,10},{9,11},{10,... | collective-permute-start | bytes 720008 | tf_op jit(solution)/shard_map/cond/branch_1_fun/ppermute | solution.py:236
  9.8 0.0 collective-permute-start.4
  9.8 10.6 %collective-permute-done.1.refs_2_ = bf16[1,80,1500]{2,1,0:T(8,128)(2,1)S(1)} collective-permute-done((bf16[1,80,1500]{2,1,0:T(8,128)(2,1)S(1)}, bf16[1,80,1500]{2,1,0:T(8,128)(2,1)S(1)}, u32[]{:S(2)}, u32[]{:S(2)}) %collective-permute-start.1) | collective-permute-done | bytes 240032 | tf_op jit(solution)/shard_map/cond/branch_1_fun/ppermute | solution.py:236
  20.5 0.6 collective-permute-done.refs_1_
  21.1 0.5 collective-permute-start.6
  21.6 1.1 %collective-permute-start.3 = (bf16[1,80,1500]{2,1,0:T(8,128)(2,1)S(1)}, bf16[1,80,1500]{2,1,0:T(8,128)(2,1)S(1)}, u32[]{:S(2)}, u32[]{:S(2)}) collective-permute-start(bf16[1,80,1500]{2,1,0:T(8,128)(2,1)S(1)} %collective-permute-done.1.refs_2_), channel_id=1, source_target_pairs={{0,2},{1,3},{2,0},{3,1},{4,6},{5,7},{6,4},{7,5},{8,10},{9,11},{10,... | collective-permute-start | bytes 720008 | tf_op jit(solution)/shard_map/cond/branch_1_fun/ppermute | solution.py:236
  22.6 1.3 %branch_1_fun.10 = (bf16[1,48,1500]{2,1,0:T(8,128)(2,1)S(1)}, bf16[1,48,1500]{2,1,0:T(8,128)(2,1)S(1)}) custom-call(s32[4]{0:T(128)S(1)} %get-tuple-element.75.offsets, bf16[1500,1024]{1,0:T(8,128)(2,1)S(1)} %get-tuple-element.76.chol.refs_8_), custom_call_target="tpu_custom_call" | custom-call | bytes 3072016 | tf_op jit(solution)/shard_map/cond/branch_1_fun/pallas_call | solution.py:184
  23.9 0.1 collective-permute-start.2
  24.0 1.4 %collective-permute-done.2 = bf16[1,48,1500]{2,1,0:T(8,128)(2,1)S(1)} collective-permute-done((bf16[1,48,1500]{2,1,0:T(8,128)(2,1)S(1)}, bf16[1,48,1500]{2,1,0:T(8,128)(2,1)S(1)}, u32[]{:S(2)}, u32[]{:S(2)}) %collective-permute-start.2) | collective-permute-done | bytes 144032 | tf_op jit(solution)/shard_map/cond/branch_1_fun/ppermute | solution.py:228
  25.4 4.0 %collective-permute-done.3.refs_3_ = bf16[1,80,1500]{2,1,0:T(8,128)(2,1)S(1)} collective-permute-done((bf16[1,80,1500]{2,1,0:T(8,128)(2,1)S(1)}, bf16[1,80,1500]{2,1,0:T(8,128)(2,1)S(1)}, u32[]{:S(2)}, u32[]{:S(2)}) %collective-permute-start.3) | collective-permute-done | bytes 240032 | tf_op jit(solution)/shard_map/cond/branch_1_fun/ppermute | solution.py:236
  29.4 1.5 %collective-permute-done.7.refs_7_ = bf16[1,80,1500]{2,1,0:T(8,128)(2,1)S(1)} collective-permute-done((bf16[1,80,1500]{2,1,0:T(8,128)(2,1)S(1)}, bf16[1,80,1500]{2,1,0:T(8,128)(2,1)S(1)}, u32[]{:S(2)}, u32[]{:S(2)}) %collective-permute-start.7) | collective-permute-done | bytes 240032 | tf_op jit(solution)/shard_map/cond/branch_1_fun/ppermute | solution.py:239
  30.9 2.2 %branch_1_fun.11.own = f32[2576,128]{1,0:T(8,128)S(1)} custom-call(s32[4]{0:T(128)S(1)} %get-tuple-element.75.offsets, bf16[1,80,1500]{2,1,0:T(8,128)(2,1)S(1)} %add.17.refs_0_, bf16[1,80,1500]{2,1,0:T(8,128)(2,1)S(1)} %collective-permute-done.refs_1_, bf16[1,80,1500]{2,1,0:T(8,128)(2,1)S(1)} %collective-permute-done.1.refs_2_, ...), custom_call_target="tpu_custom_call" | custom-call | flops 983040000 | bytes 4992016 | tf_op jit(solution)/shard_map/cond/branch_1_fun/pallas_call | solution.py:184
  33.1 0.1 convert_element_type.44
  33.2 1.6 %collective-permute-start.8 = (f16[2576,128]{1,0:T(8,128)(2,1)S(1)}, f16[2576,128]{1,0:T(8,128)(2,1)S(1)}, u32[]{:S(2)}, u32[]{:S(2)}) collective-permute-start(f16[2576,128]{1,0:T(8,128)(2,1)S(1)} %convert_element_type.44), channel_id=1, source_target_pairs={{0,8},{1,17},{2,10},{3,19},{4,12},{5,21},{6,14},{7,23},{8,0},{9,25... | collective-permute-start | bytes 1978376 | tf_op jit(solution)/shard_map/cond/branch_1_fun/ppermute | solution.py:256
  34.8 1.1 %collective-permute-start.10 = (bf16[1,48,1500]{2,1,0:T(8,128)(2,1)S(1)}, bf16[1,48,1500]{2,1,0:T(8,128)(2,1)S(1)}, u32[]{:S(2)}, u32[]{:S(2)}) collective-permute-start(bf16[1,48,1500]{2,1,0:T(8,128)(2,1)S(1)} %add.18.refs_0_), channel_id=1, source_target_pairs={{0,2},{1,3},{2,0},{3,1},{4,6},{5,7},{6,4},{7,5},{8,10},{9,11},{10,... | collective-permute-start | bytes 432008 | tf_op jit(solution)/shard_map/cond/branch_1_fun/ppermute | solution.py:236
  35.9 2.1 %collective-permute-start.9 = (bf16[1,48,1500]{2,1,0:T(8,128)(2,1)S(1)}, bf16[1,48,1500]{2,1,0:T(8,128)(2,1)S(1)}, u32[]{:S(2)}, u32[]{:S(2)}) collective-permute-start(bf16[1,48,1500]{2,1,0:T(8,128)(2,1)S(1)} %add.18.refs_0_), channel_id=1, source_target_pairs={{0,4},{1,5},{2,6},{3,7},{4,0},{5,1},{6,2},{7,3},{8,12},{9,13},{10,... | collective-permute-start | bytes 432008 | tf_op jit(solution)/shard_map/cond/branch_1_fun/ppermute | solution.py:236
  38.0 6.0 %collective-permute-done.8 = f16[2576,128]{1,0:T(8,128)(2,1)S(1)} collective-permute-done((f16[2576,128]{1,0:T(8,128)(2,1)S(1)}, f16[2576,128]{1,0:T(8,128)(2,1)S(1)}, u32[]{:S(2)}, u32[]{:S(2)}) %collective-permute-start.8) | collective-permute-done | bytes 659488 | tf_op jit(solution)/shard_map/cond/branch_1_fun/ppermute | solution.py:256
  43.9 0.1 convert_element_type.45.came
  44.0 1.3 %collective-permute-done.9.refs_2_ = bf16[1,48,1500]{2,1,0:T(8,128)(2,1)S(1)} collective-permute-done((bf16[1,48,1500]{2,1,0:T(8,128)(2,1)S(1)}, bf16[1,48,1500]{2,1,0:T(8,128)(2,1)S(1)}, u32[]{:S(2)}, u32[]{:S(2)}) %collective-permute-start.9) | collective-permute-done | bytes 144032 | tf_op jit(solution)/shard_map/cond/branch_1_fun/ppermute | solution.py:236
  45.3 0.2 branch_1_fun.12.own
  45.6 0.1 convert_element_type.46
  45.7 0.5 collective-permute-start.16
  46.2 0.8 collective-permute-start.11
  47.0 0.5 collective-permute-start.14
  47.5 4.9 %collective-permute-done.11.refs_3_ = bf16[1,48,1500]{2,1,0:T(8,128)(2,1)S(1)} collective-permute-done((bf16[1,48,1500]{2,1,0:T(8,128)(2,1)S(1)}, bf16[1,48,1500]{2,1,0:T(8,128)(2,1)S(1)}, u32[]{:S(2)}, u32[]{:S(2)}) %collective-permute-start.11) | collective-permute-done | bytes 144032 | tf_op jit(solution)/shard_map/cond/branch_1_fun/ppermute | solution.py:236
  52.5 1.3 %collective-permute-done.15.refs_7_ = bf16[1,48,1500]{2,1,0:T(8,128)(2,1)S(1)} collective-permute-done((bf16[1,48,1500]{2,1,0:T(8,128)(2,1)S(1)}, bf16[1,48,1500]{2,1,0:T(8,128)(2,1)S(1)}, u32[]{:S(2)}, u32[]{:S(2)}) %collective-permute-start.15) | collective-permute-done | bytes 144032 | tf_op jit(solution)/shard_map/cond/branch_1_fun/ppermute | solution.py:239
  53.8 1.7 %branch_1_fun.13.own = f32[1552,128]{1,0:T(8,128)S(1)} custom-call(s32[4]{0:T(128)S(1)} %get-tuple-element.75.offsets, bf16[1,48,1500]{2,1,0:T(8,128)(2,1)S(1)} %add.18.refs_0_, bf16[1,48,1500]{2,1,0:T(8,128)(2,1)S(1)} %collective-permute-done.10.refs_1_, bf16[1,48,1500]{2,1,0:T(8,128)(2,1)S(1)} %collective-permute-done.9.refs_2_, ...), custom_call_target="tpu_custom_call" | custom-call | flops 589824000 | bytes 4224016 | tf_op jit(solution)/shard_map/cond/branch_1_fun/pallas_call | solution.py:184
  55.6 0.0 copy-start.2
  55.6 0.8 collective-permute-done.16
  56.3 0.1 convert_element_type.47.came
  56.4 0.1 convert_element_type.48
  56.5 1.6 %collective-permute-start.17 = (f16[1552,128]{1,0:T(8,128)(2,1)S(1)}, f16[1552,128]{1,0:T(8,128)(2,1)S(1)}, u32[]{:S(2)}, u32[]{:S(2)}) collective-permute-start(f16[1552,128]{1,0:T(8,128)(2,1)S(1)} %convert_element_type.48), channel_id=1, source_target_pairs={{0,8},{1,17},{2,10},{3,19},{4,12},{5,21},{6,14},{7,23},{8,0},{9,25... | collective-permute-start | bytes 1191944 | tf_op jit(solution)/shard_map/cond/branch_1_fun/ppermute | solution.py:256
  58.1 1.0 %branch_1_fun.15 = (f32[4,40,1024]{2,1,0:T(8,128)S(1)}, f32[4,16,1024]{2,1,0:T(8,128)S(1)}, f32[4,16,1024]{2,1,0:T(8,128)S(1)}, f32[4,8,1024]{2,1,0:T(8,128)S(1)}) custom-call(f32[2576,128]{1,0:T(8,128)S(1)} %branch_1_fun.12.own, f32[2576,128]{1,0:T(8,128)S(1)} %convert_element_type.47.came, bf16[1024,1024]{1,0:T(8,128)(2,1)S(1)} %copy-done.2), custom_call_target="tpu_custom_call" | custom-call | flops 671088640 | bytes 4734976 | tf_op jit(solution)/shard_map/cond/branch_1_fun/pallas_call | solution.py:184
  59.1 0.1 collective-permute-start.18
  59.2 0.5 collective-permute-start.19
  59.7 0.1 collective-permute-start.20
  59.7 1.5 %collective-permute-done.20.refs_2_ = f32[4,8,1024]{2,1,0:T(8,128)S(1)} collective-permute-done((f32[4,8,1024]{2,1,0:T(8,128)S(1)}, f32[4,8,1024]{2,1,0:T(8,128)S(1)}, u32[]{:S(2)}, u32[]{:S(2)}) %collective-permute-start.20) | collective-permute-done | bytes 131104 | tf_op jit(solution)/shard_map/cond/branch_1_fun/ppermute | solution.py:239
  61.3 0.1 branch_1_fun.16
  61.3 3.1 %collective-permute-done.17 = f16[1552,128]{1,0:T(8,128)(2,1)S(1)} collective-permute-done((f16[1552,128]{1,0:T(8,128)(2,1)S(1)}, f16[1552,128]{1,0:T(8,128)(2,1)S(1)}, u32[]{:S(2)}, u32[]{:S(2)}) %collective-permute-start.17) | collective-permute-done | bytes 397344 | tf_op jit(solution)/shard_map/cond/branch_1_fun/ppermute | solution.py:256
  64.4 0.1 convert_element_type.49.came
  64.4 0.1 branch_1_fun.14.own
  64.5 0.1 convert_element_type.50
  64.6 0.5 collective-permute-start.21
  65.1 2.4 %collective-permute-start.22 = (bf16[40,1024]{1,0:T(8,128)(2,1)S(1)}, bf16[40,1024]{1,0:T(8,128)(2,1)S(1)}, u32[]{:S(2)}, u32[]{:S(2)}) collective-permute-start(bf16[40,1024]{1,0:T(8,128)(2,1)S(1)} %get-tuple-element.101), channel_id=1, source_target_pairs={{0,6},{1,7},{2,4},{3,5},{4,2},{5,3},{6,0},{7,1},{8,14},{9,15},{10,... | collective-permute-start | bytes 245768 | tf_op jit(solution)/shard_map/cond/branch_1_fun/ppermute | solution.py:292
  67.5 2.0 %collective-permute-start.24 = (bf16[40,1024]{1,0:T(8,128)(2,1)S(1)}, bf16[40,1024]{1,0:T(8,128)(2,1)S(1)}, u32[]{:S(2)}, u32[]{:S(2)}) collective-permute-start(bf16[40,1024]{1,0:T(8,128)(2,1)S(1)} %get-tuple-element.103), channel_id=1, source_target_pairs={{0,2},{1,3},{2,0},{3,1},{4,6},{5,7},{6,4},{7,5},{8,10},{9,11},{10,... | collective-permute-start | bytes 245768 | tf_op jit(solution)/shard_map/cond/branch_1_fun/ppermute | solution.py:292
  69.5 3.0 %collective-permute-done.21 = f16[1552,128]{1,0:T(8,128)(2,1)S(1)} collective-permute-done((f16[1552,128]{1,0:T(8,128)(2,1)S(1)}, f16[1552,128]{1,0:T(8,128)(2,1)S(1)}, u32[]{:S(2)}, u32[]{:S(2)}) %collective-permute-start.21) | collective-permute-done | bytes 397344 | tf_op jit(solution)/shard_map/cond/branch_1_fun/ppermute | solution.py:256
  72.5 0.1 convert_element_type.51.came
  72.6 1.9 %collective-permute-done.23.refs_2_ = bf16[40,1024]{1,0:T(8,128)(2,1)S(1)} collective-permute-done((bf16[40,1024]{1,0:T(8,128)(2,1)S(1)}, bf16[40,1024]{1,0:T(8,128)(2,1)S(1)}, u32[]{:S(2)}, u32[]{:S(2)}) %collective-permute-start.23) | collective-permute-done | bytes 81952 | tf_op jit(solution)/shard_map/cond/branch_1_fun/ppermute | solution.py:292
  74.5 0.7 branch_1_fun.17
  75.2 0.1 collective-permute-start.25
  75.3 1.7 %collective-permute-done.25.refs_0_ = f32[4,24,1024]{2,1,0:T(8,128)S(1)} collective-permute-done((f32[4,24,1024]{2,1,0:T(8,128)S(1)}, f32[4,24,1024]{2,1,0:T(8,128)S(1)}, u32[]{:S(2)}, u32[]{:S(2)}) %collective-permute-start.25) | collective-permute-done | bytes 393248 | tf_op jit(solution)/shard_map/cond/branch_1_fun/ppermute | solution.py:239
  77.1 1.9 %collective-permute-start.26 = (bf16[24,1024]{1,0:T(8,128)(2,1)S(1)}, bf16[24,1024]{1,0:T(8,128)(2,1)S(1)}, u32[]{:S(2)}, u32[]{:S(2)}) collective-permute-start(bf16[24,1024]{1,0:T(8,128)(2,1)S(1)} %get-tuple-element.112), channel_id=1, source_target_pairs={{0,6},{1,7},{2,4},{3,5},{4,2},{5,3},{6,0},{7,1},{8,14},{9,15},{10,... | collective-permute-start | bytes 147464 | tf_op jit(solution)/shard_map/cond/branch_1_fun/ppermute | solution.py:292
  78.9 2.6 %collective-permute-start.28 = (bf16[24,1024]{1,0:T(8,128)(2,1)S(1)}, bf16[24,1024]{1,0:T(8,128)(2,1)S(1)}, u32[]{:S(2)}, u32[]{:S(2)}) collective-permute-start(bf16[24,1024]{1,0:T(8,128)(2,1)S(1)} %get-tuple-element.114), channel_id=1, source_target_pairs={{0,2},{1,3},{2,0},{3,1},{4,6},{5,7},{6,4},{7,5},{8,10},{9,11},{10,... | collective-permute-start | bytes 147464 | tf_op jit(solution)/shard_map/cond/branch_1_fun/ppermute | solution.py:292
  81.5 1.8 %collective-permute-done.26.refs_5_ = bf16[24,1024]{1,0:T(8,128)(2,1)S(1)} collective-permute-done((bf16[24,1024]{1,0:T(8,128)(2,1)S(1)}, bf16[24,1024]{1,0:T(8,128)(2,1)S(1)}, u32[]{:S(2)}, u32[]{:S(2)}) %collective-permute-start.26) | collective-permute-done | bytes 49184 | tf_op jit(solution)/shard_map/cond/branch_1_fun/ppermute | solution.py:292
  83.4 1.5 %collective-permute-done.27.refs_6_ = bf16[24,1024]{1,0:T(8,128)(2,1)S(1)} collective-permute-done((bf16[24,1024]{1,0:T(8,128)(2,1)S(1)}, bf16[24,1024]{1,0:T(8,128)(2,1)S(1)}, u32[]{:S(2)}, u32[]{:S(2)}) %collective-permute-start.27) | collective-permute-done | bytes 49184 | tf_op jit(solution)/shard_map/cond/branch_1_fun/ppermute | solution.py:292
  84.8 0.1 branch_1_fun.19
  85.1 0.0 copy-start.3
  85.1 0.7 copy-done.3
  (26 shorter events, 0.1 us)
Async XLA Ops:
  0.0 4.6 %copy-start.4 = (s32[4]{0:T(128)S(1)}, s32[4]{0:T(128)}, u32[]{:S(2)}) copy-start(s32[4]{0:T(128)} %offsets.1) | copy-start | bytes 52
  0.0 4.6 %copy-start = (bf16[1500,1024]{1,0:T(8,128)(2,1)S(1)}, bf16[1500,1024]{1,0:T(8,128)(2,1)}, u32[]{:S(2)}) copy-start(bf16[1500,1024]{1,0:T(8,128)(2,1)} %chol.1) | copy-start | bytes 9216004
  3.0 1.6 %collective-permute-start.61 = (bf16[1,80,1500]{2,1,0:T(8,128)(2,1)S(1)}, bf16[1,80,1500]{2,1,0:T(8,128)(2,1)S(1)}, u32[]{:S(2)}, u32[]{:S(2)}) collective-permute-start(bf16[1,80,1500]{2,1,0:T(8,128)(2,1)S(1)} %get-tuple-element.120), channel_id=1, source_target_pairs={{0,1},{1,0},{2,3},{3,2},{4,5},{5,4},{6,7},{7,6},{8,9},{9,8},{10,11... | collective-permute-start | bytes 720008 | tf_op jit(solution)/shard_map/ppermute | solution.py:228
  4.7 15.8 %collective-permute-start.1 = (bf16[1,80,1500]{2,1,0:T(8,128)(2,1)S(1)}, bf16[1,80,1500]{2,1,0:T(8,128)(2,1)S(1)}, u32[]{:S(2)}, u32[]{:S(2)}) collective-permute-start(bf16[1,80,1500]{2,1,0:T(8,128)(2,1)S(1)} %add.17.refs_0_), channel_id=1, source_target_pairs={{0,4},{1,5},{2,6},{3,7},{4,0},{5,1},{6,2},{7,3},{8,12},{9,13},{10,... | collective-permute-start | bytes 720008 | tf_op jit(solution)/shard_map/cond/branch_1_fun/ppermute | solution.py:236
  8.6 12.4 %collective-permute-start = (bf16[1,80,1500]{2,1,0:T(8,128)(2,1)S(1)}, bf16[1,80,1500]{2,1,0:T(8,128)(2,1)S(1)}, u32[]{:S(2)}, u32[]{:S(2)}) collective-permute-start(bf16[1,80,1500]{2,1,0:T(8,128)(2,1)S(1)} %add.17.refs_0_), channel_id=1, source_target_pairs={{0,2},{1,3},{2,0},{3,1},{4,6},{5,7},{6,4},{7,5},{8,10},{9,11},{10,... | collective-permute-start | bytes 720008 | tf_op jit(solution)/shard_map/cond/branch_1_fun/ppermute | solution.py:236
  9.8 15.6 %collective-permute-start.4 = (bf16[1,80,1500]{2,1,0:T(8,128)(2,1)S(1)}, bf16[1,80,1500]{2,1,0:T(8,128)(2,1)S(1)}, u32[]{:S(2)}, u32[]{:S(2)}) collective-permute-start(bf16[1,80,1500]{2,1,0:T(8,128)(2,1)S(1)} %add.17.refs_0_), channel_id=1, source_target_pairs={{0,1},{1,0},{2,3},{3,2},{4,5},{5,4},{6,7},{7,6},{8,9},{9,8},{10,11... | collective-permute-start | bytes 720008 | tf_op jit(solution)/shard_map/cond/branch_1_fun/ppermute | solution.py:239
  21.0 4.4 %collective-permute-start.5 = (bf16[1,80,1500]{2,1,0:T(8,128)(2,1)S(1)}, bf16[1,80,1500]{2,1,0:T(8,128)(2,1)S(1)}, u32[]{:S(2)}, u32[]{:S(2)}) collective-permute-start(bf16[1,80,1500]{2,1,0:T(8,128)(2,1)S(1)} %collective-permute-done.refs_1_), channel_id=1, source_target_pairs={{0,1},{1,0},{2,3},{3,2},{4,5},{5,4},{6,7},{7,6},{8,9},{9,8},{10,11... | collective-permute-start | bytes 720008 | tf_op jit(solution)/shard_map/cond/branch_1_fun/ppermute | solution.py:239
  21.1 4.4 %collective-permute-start.6 = (bf16[1,80,1500]{2,1,0:T(8,128)(2,1)S(1)}, bf16[1,80,1500]{2,1,0:T(8,128)(2,1)S(1)}, u32[]{:S(2)}, u32[]{:S(2)}) collective-permute-start(bf16[1,80,1500]{2,1,0:T(8,128)(2,1)S(1)} %collective-permute-done.1.refs_2_), channel_id=1, source_target_pairs={{0,1},{1,0},{2,3},{3,2},{4,5},{5,4},{6,7},{7,6},{8,9},{9,8},{10,11... | collective-permute-start | bytes 720008 | tf_op jit(solution)/shard_map/cond/branch_1_fun/ppermute | solution.py:239
  21.6 7.9 %collective-permute-start.3 = (bf16[1,80,1500]{2,1,0:T(8,128)(2,1)S(1)}, bf16[1,80,1500]{2,1,0:T(8,128)(2,1)S(1)}, u32[]{:S(2)}, u32[]{:S(2)}) collective-permute-start(bf16[1,80,1500]{2,1,0:T(8,128)(2,1)S(1)} %collective-permute-done.1.refs_2_), channel_id=1, source_target_pairs={{0,2},{1,3},{2,0},{3,1},{4,6},{5,7},{6,4},{7,5},{8,10},{9,11},{10,... | collective-permute-start | bytes 720008 | tf_op jit(solution)/shard_map/cond/branch_1_fun/ppermute | solution.py:236
  23.9 1.4 %collective-permute-start.2 = (bf16[1,48,1500]{2,1,0:T(8,128)(2,1)S(1)}, bf16[1,48,1500]{2,1,0:T(8,128)(2,1)S(1)}, u32[]{:S(2)}, u32[]{:S(2)}) collective-permute-start(bf16[1,48,1500]{2,1,0:T(8,128)(2,1)S(1)} %get-tuple-element.78), channel_id=1, source_target_pairs={{0,1},{1,0},{2,3},{3,2},{4,5},{5,4},{6,7},{7,6},{8,9},{9,8},{10,11... | collective-permute-start | bytes 432008 | tf_op jit(solution)/shard_map/cond/branch_1_fun/ppermute | solution.py:228
  29.4 1.5 %collective-permute-start.7 = (bf16[1,80,1500]{2,1,0:T(8,128)(2,1)S(1)}, bf16[1,80,1500]{2,1,0:T(8,128)(2,1)S(1)}, u32[]{:S(2)}, u32[]{:S(2)}) collective-permute-start(bf16[1,80,1500]{2,1,0:T(8,128)(2,1)S(1)} %collective-permute-done.3.refs_3_), channel_id=1, source_target_pairs={{0,1},{1,0},{2,3},{3,2},{4,5},{5,4},{6,7},{7,6},{8,9},{9,8},{10,11... | collective-permute-start | bytes 720008 | tf_op jit(solution)/shard_map/cond/branch_1_fun/ppermute | solution.py:239
  33.2 10.7 %collective-permute-start.8 = (f16[2576,128]{1,0:T(8,128)(2,1)S(1)}, f16[2576,128]{1,0:T(8,128)(2,1)S(1)}, u32[]{:S(2)}, u32[]{:S(2)}) collective-permute-start(f16[2576,128]{1,0:T(8,128)(2,1)S(1)} %convert_element_type.44), channel_id=1, source_target_pairs={{0,8},{1,17},{2,10},{3,19},{4,12},{5,21},{6,14},{7,23},{8,0},{9,25... | collective-permute-start | bytes 1978376 | tf_op jit(solution)/shard_map/cond/branch_1_fun/ppermute | solution.py:256
  34.8 9.2 %collective-permute-start.10 = (bf16[1,48,1500]{2,1,0:T(8,128)(2,1)S(1)}, bf16[1,48,1500]{2,1,0:T(8,128)(2,1)S(1)}, u32[]{:S(2)}, u32[]{:S(2)}) collective-permute-start(bf16[1,48,1500]{2,1,0:T(8,128)(2,1)S(1)} %add.18.refs_0_), channel_id=1, source_target_pairs={{0,2},{1,3},{2,0},{3,1},{4,6},{5,7},{6,4},{7,5},{8,10},{9,11},{10,... | collective-permute-start | bytes 432008 | tf_op jit(solution)/shard_map/cond/branch_1_fun/ppermute | solution.py:236
  35.9 9.5 %collective-permute-start.9 = (bf16[1,48,1500]{2,1,0:T(8,128)(2,1)S(1)}, bf16[1,48,1500]{2,1,0:T(8,128)(2,1)S(1)}, u32[]{:S(2)}, u32[]{:S(2)}) collective-permute-start(bf16[1,48,1500]{2,1,0:T(8,128)(2,1)S(1)} %add.18.refs_0_), channel_id=1, source_target_pairs={{0,4},{1,5},{2,6},{3,7},{4,0},{5,1},{6,2},{7,3},{8,12},{9,13},{10,... | collective-permute-start | bytes 432008 | tf_op jit(solution)/shard_map/cond/branch_1_fun/ppermute | solution.py:236
  45.7 10.7 %collective-permute-start.16 = (f16[2576,128]{1,0:T(8,128)(2,1)S(1)}, f16[2576,128]{1,0:T(8,128)(2,1)S(1)}, u32[]{:S(2)}, u32[]{:S(2)}) collective-permute-start(f16[2576,128]{1,0:T(8,128)(2,1)S(1)} %convert_element_type.46), channel_id=1, source_target_pairs={{0,16},{1,9},{2,18},{3,11},{4,20},{5,13},{6,22},{7,15},{8,24},{9,1... | collective-permute-start | bytes 1978376 | tf_op jit(solution)/shard_map/cond/branch_1_fun/ppermute | solution.py:256
  46.2 6.3 %collective-permute-start.11 = (bf16[1,48,1500]{2,1,0:T(8,128)(2,1)S(1)}, bf16[1,48,1500]{2,1,0:T(8,128)(2,1)S(1)}, u32[]{:S(2)}, u32[]{:S(2)}) collective-permute-start(bf16[1,48,1500]{2,1,0:T(8,128)(2,1)S(1)} %collective-permute-done.9.refs_2_), channel_id=1, source_target_pairs={{0,2},{1,3},{2,0},{3,1},{4,6},{5,7},{6,4},{7,5},{8,10},{9,11},{10,... | collective-permute-start | bytes 432008 | tf_op jit(solution)/shard_map/cond/branch_1_fun/ppermute | solution.py:236
  47.0 5.5 %collective-permute-start.12 = (bf16[1,48,1500]{2,1,0:T(8,128)(2,1)S(1)}, bf16[1,48,1500]{2,1,0:T(8,128)(2,1)S(1)}, u32[]{:S(2)}, u32[]{:S(2)}) collective-permute-start(bf16[1,48,1500]{2,1,0:T(8,128)(2,1)S(1)} %add.18.refs_0_), channel_id=1, source_target_pairs={{0,1},{1,0},{2,3},{3,2},{4,5},{5,4},{6,7},{7,6},{8,9},{9,8},{10,11... | collective-permute-start | bytes 432008 | tf_op jit(solution)/shard_map/cond/branch_1_fun/ppermute | solution.py:239
  47.0 5.5 %collective-permute-start.14 = (bf16[1,48,1500]{2,1,0:T(8,128)(2,1)S(1)}, bf16[1,48,1500]{2,1,0:T(8,128)(2,1)S(1)}, u32[]{:S(2)}, u32[]{:S(2)}) collective-permute-start(bf16[1,48,1500]{2,1,0:T(8,128)(2,1)S(1)} %collective-permute-done.9.refs_2_), channel_id=1, source_target_pairs={{0,1},{1,0},{2,3},{3,2},{4,5},{5,4},{6,7},{7,6},{8,9},{9,8},{10,11... | collective-permute-start | bytes 432008 | tf_op jit(solution)/shard_map/cond/branch_1_fun/ppermute | solution.py:239
  47.5 5.0 %collective-permute-start.13 = (bf16[1,48,1500]{2,1,0:T(8,128)(2,1)S(1)}, bf16[1,48,1500]{2,1,0:T(8,128)(2,1)S(1)}, u32[]{:S(2)}, u32[]{:S(2)}) collective-permute-start(bf16[1,48,1500]{2,1,0:T(8,128)(2,1)S(1)} %collective-permute-done.10.refs_1_), channel_id=1, source_target_pairs={{0,1},{1,0},{2,3},{3,2},{4,5},{5,4},{6,7},{7,6},{8,9},{9,8},{10,11... | collective-permute-start | bytes 432008 | tf_op jit(solution)/shard_map/cond/branch_1_fun/ppermute | solution.py:239
  52.5 1.4 %collective-permute-start.15 = (bf16[1,48,1500]{2,1,0:T(8,128)(2,1)S(1)}, bf16[1,48,1500]{2,1,0:T(8,128)(2,1)S(1)}, u32[]{:S(2)}, u32[]{:S(2)}) collective-permute-start(bf16[1,48,1500]{2,1,0:T(8,128)(2,1)S(1)} %collective-permute-done.11.refs_3_), channel_id=1, source_target_pairs={{0,1},{1,0},{2,3},{3,2},{4,5},{5,4},{6,7},{7,6},{8,9},{9,8},{10,11... | collective-permute-start | bytes 432008 | tf_op jit(solution)/shard_map/cond/branch_1_fun/ppermute | solution.py:239
  55.6 2.5 %copy-start.2 = (bf16[1024,1024]{1,0:T(8,128)(2,1)S(1)}, bf16[1024,1024]{1,0:T(8,128)(2,1)}, u32[]{:S(2)}) copy-start(bf16[1024,1024]{1,0:T(8,128)(2,1)} %get-tuple-element.90.amplitudes) | copy-start | bytes 6291460 | tf_op jit(solution)/shard_map/cond
  56.5 7.9 %collective-permute-start.17 = (f16[1552,128]{1,0:T(8,128)(2,1)S(1)}, f16[1552,128]{1,0:T(8,128)(2,1)S(1)}, u32[]{:S(2)}, u32[]{:S(2)}) collective-permute-start(f16[1552,128]{1,0:T(8,128)(2,1)S(1)} %convert_element_type.48), channel_id=1, source_target_pairs={{0,8},{1,17},{2,10},{3,19},{4,12},{5,21},{6,14},{7,23},{8,0},{9,25... | collective-permute-start | bytes 1191944 | tf_op jit(solution)/shard_map/cond/branch_1_fun/ppermute | solution.py:256
  59.1 2.2 %collective-permute-start.18 = (f32[4,16,1024]{2,1,0:T(8,128)S(1)}, f32[4,16,1024]{2,1,0:T(8,128)S(1)}, u32[]{:S(2)}, u32[]{:S(2)}) collective-permute-start(f32[4,16,1024]{2,1,0:T(8,128)S(1)} %get-tuple-element.92), channel_id=1, source_target_pairs={{0,1},{1,0},{2,3},{3,2},{4,5},{5,4},{6,7},{7,6},{8,9},{9,8},{10,11... | collective-permute-start | bytes 786440 | tf_op jit(solution)/shard_map/cond/branch_1_fun/ppermute | solution.py:239
  59.2 2.1 %collective-permute-start.19 = (f32[4,16,1024]{2,1,0:T(8,128)S(1)}, f32[4,16,1024]{2,1,0:T(8,128)S(1)}, u32[]{:S(2)}, u32[]{:S(2)}) collective-permute-start(f32[4,16,1024]{2,1,0:T(8,128)S(1)} %get-tuple-element.93), channel_id=1, source_target_pairs={{0,1},{1,0},{2,3},{3,2},{4,5},{5,4},{6,7},{7,6},{8,9},{9,8},{10,11... | collective-permute-start | bytes 786440 | tf_op jit(solution)/shard_map/cond/branch_1_fun/ppermute | solution.py:239
  59.7 1.6 %collective-permute-start.20 = (f32[4,8,1024]{2,1,0:T(8,128)S(1)}, f32[4,8,1024]{2,1,0:T(8,128)S(1)}, u32[]{:S(2)}, u32[]{:S(2)}) collective-permute-start(f32[4,8,1024]{2,1,0:T(8,128)S(1)} %get-tuple-element.94), channel_id=1, source_target_pairs={{0,1},{1,0},{2,3},{3,2},{4,5},{5,4},{6,7},{7,6},{8,9},{9,8},{10,11... | collective-permute-start | bytes 393224 | tf_op jit(solution)/shard_map/cond/branch_1_fun/ppermute | solution.py:239
  64.6 7.9 %collective-permute-start.21 = (f16[1552,128]{1,0:T(8,128)(2,1)S(1)}, f16[1552,128]{1,0:T(8,128)(2,1)S(1)}, u32[]{:S(2)}, u32[]{:S(2)}) collective-permute-start(f16[1552,128]{1,0:T(8,128)(2,1)S(1)} %convert_element_type.50), channel_id=1, source_target_pairs={{0,16},{1,9},{2,18},{3,11},{4,20},{5,13},{6,22},{7,15},{8,24},{9,1... | collective-permute-start | bytes 1191944 | tf_op jit(solution)/shard_map/cond/branch_1_fun/ppermute | solution.py:256
  65.1 7.4 %collective-permute-start.22 = (bf16[40,1024]{1,0:T(8,128)(2,1)S(1)}, bf16[40,1024]{1,0:T(8,128)(2,1)S(1)}, u32[]{:S(2)}, u32[]{:S(2)}) collective-permute-start(bf16[40,1024]{1,0:T(8,128)(2,1)S(1)} %get-tuple-element.101), channel_id=1, source_target_pairs={{0,6},{1,7},{2,4},{3,5},{4,2},{5,3},{6,0},{7,1},{8,14},{9,15},{10,... | collective-permute-start | bytes 245768 | tf_op jit(solution)/shard_map/cond/branch_1_fun/ppermute | solution.py:292
  67.5 7.0 %collective-permute-start.23 = (bf16[40,1024]{1,0:T(8,128)(2,1)S(1)}, bf16[40,1024]{1,0:T(8,128)(2,1)S(1)}, u32[]{:S(2)}, u32[]{:S(2)}) collective-permute-start(bf16[40,1024]{1,0:T(8,128)(2,1)S(1)} %get-tuple-element.102), channel_id=1, source_target_pairs={{0,4},{1,5},{2,6},{3,7},{4,0},{5,1},{6,2},{7,3},{8,12},{9,13},{10,... | collective-permute-start | bytes 245768 | tf_op jit(solution)/shard_map/cond/branch_1_fun/ppermute | solution.py:292
  67.5 7.0 %collective-permute-start.24 = (bf16[40,1024]{1,0:T(8,128)(2,1)S(1)}, bf16[40,1024]{1,0:T(8,128)(2,1)S(1)}, u32[]{:S(2)}, u32[]{:S(2)}) collective-permute-start(bf16[40,1024]{1,0:T(8,128)(2,1)S(1)} %get-tuple-element.103), channel_id=1, source_target_pairs={{0,2},{1,3},{2,0},{3,1},{4,6},{5,7},{6,4},{7,5},{8,10},{9,11},{10,... | collective-permute-start | bytes 245768 | tf_op jit(solution)/shard_map/cond/branch_1_fun/ppermute | solution.py:292
  75.2 1.8 %collective-permute-start.25 = (f32[4,24,1024]{2,1,0:T(8,128)S(1)}, f32[4,24,1024]{2,1,0:T(8,128)S(1)}, u32[]{:S(2)}, u32[]{:S(2)}) collective-permute-start(f32[4,24,1024]{2,1,0:T(8,128)S(1)} %get-tuple-element.110), channel_id=1, source_target_pairs={{0,1},{1,0},{2,3},{3,2},{4,5},{5,4},{6,7},{7,6},{8,9},{9,8},{10,11... | collective-permute-start | bytes 1179656 | tf_op jit(solution)/shard_map/cond/branch_1_fun/ppermute | solution.py:239
  77.1 6.3 %collective-permute-start.26 = (bf16[24,1024]{1,0:T(8,128)(2,1)S(1)}, bf16[24,1024]{1,0:T(8,128)(2,1)S(1)}, u32[]{:S(2)}, u32[]{:S(2)}) collective-permute-start(bf16[24,1024]{1,0:T(8,128)(2,1)S(1)} %get-tuple-element.112), channel_id=1, source_target_pairs={{0,6},{1,7},{2,4},{3,5},{4,2},{5,3},{6,0},{7,1},{8,14},{9,15},{10,... | collective-permute-start | bytes 147464 | tf_op jit(solution)/shard_map/cond/branch_1_fun/ppermute | solution.py:292
  78.9 5.9 %collective-permute-start.27 = (bf16[24,1024]{1,0:T(8,128)(2,1)S(1)}, bf16[24,1024]{1,0:T(8,128)(2,1)S(1)}, u32[]{:S(2)}, u32[]{:S(2)}) collective-permute-start(bf16[24,1024]{1,0:T(8,128)(2,1)S(1)} %get-tuple-element.113), channel_id=1, source_target_pairs={{0,4},{1,5},{2,6},{3,7},{4,0},{5,1},{6,2},{7,3},{8,12},{9,13},{10,... | collective-permute-start | bytes 147464 | tf_op jit(solution)/shard_map/cond/branch_1_fun/ppermute | solution.py:292
  78.9 5.9 %collective-permute-start.28 = (bf16[24,1024]{1,0:T(8,128)(2,1)S(1)}, bf16[24,1024]{1,0:T(8,128)(2,1)S(1)}, u32[]{:S(2)}, u32[]{:S(2)}) collective-permute-start(bf16[24,1024]{1,0:T(8,128)(2,1)S(1)} %get-tuple-element.114), channel_id=1, source_target_pairs={{0,2},{1,3},{2,0},{3,1},{4,6},{5,7},{6,4},{7,5},{8,10},{9,11},{10,... | collective-permute-start | bytes 147464 | tf_op jit(solution)/shard_map/cond/branch_1_fun/ppermute | solution.py:292
  85.1 0.7 copy-start.3
